TPU v7x, 32 devices: a whole 2x2x4 slice. The times are simulated.
32 devices in a mesh: dp: 8 (over z, y), head: 4 (over x, core).
Axes of the slice: x: 2, y: 2, z: 4, core: 2. Of those that a mesh axis runs over, the one named last changes fastest.
Arguments:
- tokens: bfloat16 [24, 1024, 768], P('dp', 'head'), may hold values from -6 to 6
- lengths: int32 [24, 3], P('dp'), may hold values from 0 to 1024, as said below
- w_qkv: bfloat16 [768, 2304], replicated, may hold values from -0.21875 to 0.21875
- b_qkv: bfloat16 [2304], replicated, may hold values from -3 to 3
- w_out: bfloat16 [768, 768], replicated, may hold values from -1.25 to 1.25
- b_out: bfloat16 [768], replicated, may hold values from -2 to 2
- w_in: bfloat16 [768, 3072], replicated, may hold values from -0.21875 to 0.21875
- b_in: bfloat16 [3072], replicated, may hold values from -3 to 3
- w_down: bfloat16 [3072, 768], replicated, may hold values from -0.109375 to 0.109375
- b_down: bfloat16 [768], replicated, may hold values from -2 to 2
- norm1_gain: bfloat16 [768], replicated, may hold values from 0.099609375 to 1.8984375
- norm1_bias: bfloat16 [768], replicated, may hold values from -2 to 2
- norm2_gain: bfloat16 [768], replicated, may hold values from 0.099609375 to 1.8984375
- norm2_bias: bfloat16 [768], replicated, may hold values from -2 to 2
- cotangent: bfloat16 [24, 1024, 768], P('dp', 'head'), may hold values from -6 to 6
Outputs:
- output: bfloat16 [24, 1024, 768], P('dp', 'head')
- grad_tokens: bfloat16 [24, 1024, 768], P('dp', 'head')
- grad_w_qkv: float32 [768, 2304], replicated
- grad_b_qkv: float32 [2304], replicated
- grad_w_out: float32 [768, 768], replicated
- grad_b_out: float32 [768], replicated
- grad_w_in: float32 [768, 3072], replicated
- grad_b_in: float32 [3072], replicated
- grad_w_down: float32 [3072, 768], replicated
- grad_b_down: float32 [768], replicated
- grad_norm1_gain: float32 [768], replicated
- grad_norm1_bias: float32 [768], replicated
- grad_norm2_gain: float32 [768], replicated
- grad_norm2_bias: float32 [768], replicated
Inputs may be any that keep to these rules, and one draw needn't show every extreme that they name: `lengths`: each row holds three slots (a sequence before, a main one, a sequence after); a side slot is 0 or from 32 to 127; the three sum to 1024.
All inputs are finite; a program needn't handle non-finite values.
Results may differ from a plain program's by a relative error of at most 0.0099.
Values may be sent and summed in bfloat16 or wider, within the bound.
No kernel may reach another device: no remote copies, remote signals or barrier semaphores. Data moves between devices by JAX's collectives and lax.ppermute only.
A program may use at most 192 MiB of HBM per device.

v0:
```python
import math

import jax
import jax.numpy as jnp
from jax import lax
from jax.sharding import PartitionSpec as P

HEADS = 12


def layer_norm(values, gain_row, shift_row):
    center = values - jnp.mean(values, axis=-1, keepdims=True)
    spread = jnp.mean(center * center, axis=-1, keepdims=True)
    return center * lax.rsqrt(spread + 1e-05) * gain_row + shift_row


def rotary(values, places):
    rot_width = values.shape[-1] // 4
    half_width = rot_width // 2
    frequency = 1.0 / 10000.0 ** (jnp.arange(half_width, dtype=jnp.float32) * 2.0 / rot_width)
    angles = places[..., None] * frequency
    angles = jnp.concatenate([angles, angles], axis=-1)
    turned = values[..., :rot_width]
    swapped = jnp.concatenate([-turned[..., half_width:], turned[..., :half_width]], axis=-1)
    rotated = turned * jnp.cos(angles) + swapped * jnp.sin(angles)
    return jnp.concatenate([rotated, values[..., rot_width:]], axis=-1)


def segments(lengths, places):
    first_end = lengths[:, 0:1]
    second_end = first_end + lengths[:, 1:2]
    segment = (places[None, :] >= first_end).astype(jnp.int32) + (
        places[None, :] >= second_end
    ).astype(jnp.int32)
    seg_start = jnp.where(segment == 0, 0, jnp.where(segment == 1, first_end, second_end))
    return (segment, places[None, :] - seg_start)


def inner(left_mat, right_mat):
    return lax.dot_general(
        left_mat, right_mat, (((0,), (0,)), ((), ())), preferred_element_type=jnp.float32
    )


def through(left_mat, right_mat):
    return lax.dot_general(
        left_mat, right_mat, (((1,), (1,)), ((), ())), preferred_element_type=jnp.float32
    )


def gelu_exact(values):
    return jax.nn.gelu(values, approximate=False)


def on_device(
    tokens,
    lengths,
    w_qkv,
    b_qkv,
    w_out,
    b_out,
    w_in,
    b_in,
    w_down,
    b_down,
    norm1_gain,
    norm1_bias,
    norm2_gain,
    norm2_bias,
    cotangent,
):
    row_count, span_len, model_width = tokens.shape
    groups = lax.axis_size("head")
    row_len = span_len * groups
    head_width = model_width // HEADS
    local_heads = HEADS // groups
    factor = 1.0 / math.sqrt(head_width)
    span_rows = min(512, row_len)
    whole = jnp.arange(row_len, dtype=jnp.int32)
    segment = segments(lengths, whole)[0]
    own_places = lax.axis_index("head") * span_len + jnp.arange(span_len, dtype=jnp.int32)
    angles_in = segments(lengths, own_places)[1][:, :, None].astype(jnp.float32)
    gain_one = norm1_gain.astype(jnp.float32)
    shift_one = norm1_bias.astype(jnp.float32)
    gain_two = norm2_gain.astype(jnp.float32)
    shift_two = norm2_bias.astype(jnp.float32)
    resid_flat = tokens.astype(jnp.float32).reshape(-1, model_width)
    normed_f32, norm_back_one = jax.vjp(layer_norm, resid_flat, gain_one, shift_one)
    normed = normed_f32.astype(jnp.bfloat16)
    qkv_lin = jnp.dot(normed, w_qkv, preferred_element_type=jnp.float32) + b_qkv.astype(jnp.float32)
    qkv_lin = qkv_lin.reshape(row_count, span_len, HEADS, 3, head_width)

    def turn_fn(values):
        return rotary(values, angles_in)

    packed = jnp.stack(
        [turn_fn(qkv_lin[:, :, :, 0]), turn_fn(qkv_lin[:, :, :, 1]), qkv_lin[:, :, :, 2]], axis=3
    )
    packed = packed.astype(jnp.bfloat16).reshape(
        row_count, span_len, groups, local_heads * 3 * head_width
    )
    arrived = lax.all_to_all(packed, "head", split_axis=2, concat_axis=1, tiled=True).reshape(
        row_count, row_len, local_heads, 3, head_width
    )
    q_heads = arrived[:, :, :, 0]
    k_heads = arrived[:, :, :, 1]
    v_heads = arrived[:, :, :, 2]

    def scored(start):
        q_block = q_heads[:, start : start + span_rows]
        raw = (
            jnp.einsum("rqhd,rkhd->rhqk", q_block, k_heads, preferred_element_type=jnp.float32)
            * factor
        )
        same_seg = segment[:, start : start + span_rows, None] == segment[:, None, :]
        causal = whole[None, None, :] <= whole[start : start + span_rows][None, :, None]
        return (jnp.where((same_seg & causal)[:, None], raw, -1000000000.0), q_block)

    context_parts = []
    total_parts = []
    for start in range(0, row_len, span_rows):
        raw_scores = scored(start)[0]
        row_top = jnp.max(raw_scores, axis=-1, keepdims=True)
        exp_scores = jnp.exp(raw_scores - row_top)
        row_total = jnp.sum(exp_scores, axis=-1, keepdims=True)
        prob_block = (exp_scores / row_total).astype(jnp.bfloat16)
        total_parts.append(row_top[..., 0] + jnp.log(row_total[..., 0]))
        context_parts.append(
            jnp.einsum("rhqk,rkhd->rqhd", prob_block, v_heads, preferred_element_type=jnp.float32)
        )
    context_heads = jnp.concatenate(context_parts, axis=1).astype(jnp.bfloat16)
    log_total = jnp.concatenate(total_parts, axis=2)
    context = lax.all_to_all(
        context_heads.reshape(row_count, row_len, 1, local_heads * head_width),
        "head",
        split_axis=1,
        concat_axis=2,
        tiled=True,
    )
    context = context.reshape(row_count * span_len, model_width)
    attn_out = jnp.dot(context, w_out, preferred_element_type=jnp.float32) + b_out.astype(
        jnp.float32
    )
    hidden_f32, norm_back_two = jax.vjp(layer_norm, resid_flat, gain_two, shift_two)
    hidden = hidden_f32.astype(jnp.bfloat16)
    pre_act = jnp.dot(hidden, w_in, preferred_element_type=jnp.float32) + b_in.astype(jnp.float32)
    activated_f32, gelu_back = jax.vjp(gelu_exact, pre_act)
    activated = activated_f32.astype(jnp.bfloat16)
    mlp_out = jnp.dot(activated, w_down, preferred_element_type=jnp.float32) + b_down.astype(
        jnp.float32
    )
    output = (
        (resid_flat + attn_out + mlp_out)
        .reshape(row_count, span_len, model_width)
        .astype(jnp.bfloat16)
    )
    grad_flat = cotangent.reshape(-1, model_width)
    grad_f32 = grad_flat.astype(jnp.float32)
    d_out_w = inner(context, grad_flat)
    d_bias_out = jnp.sum(grad_f32, axis=0)
    d_context = through(grad_flat, w_out).astype(jnp.bfloat16)
    d_down_w = inner(activated, grad_flat)
    d_act = through(grad_flat, w_down)
    d_pre = gelu_back(d_act)[0].astype(jnp.bfloat16)
    d_in_w = inner(hidden, d_pre)
    d_in_b = jnp.sum(d_pre.astype(jnp.float32), axis=0)
    d_hidden = through(d_pre, w_in)
    dx_two, d_gain_two, d_shift_two = norm_back_two(d_hidden)
    grad_heads = lax.all_to_all(
        d_context.reshape(row_count, span_len, groups, local_heads * head_width),
        "head",
        split_axis=2,
        concat_axis=1,
        tiled=True,
    )
    grad_heads = grad_heads.reshape(row_count, row_len, local_heads, head_width)
    d_query_parts = []
    d_keys = jnp.zeros((row_count, row_len, local_heads, head_width), jnp.float32)
    d_values = jnp.zeros((row_count, row_len, local_heads, head_width), jnp.float32)
    for start in range(0, row_len, span_rows):
        raw_scores, q_block = scored(start)
        probs = jnp.exp(raw_scores - log_total[:, :, start : start + span_rows, None])
        grad_block = grad_heads[:, start : start + span_rows]
        d_prob = jnp.einsum(
            "rqhd,rkhd->rhqk", grad_block, v_heads, preferred_element_type=jnp.float32
        )
        d_scores = (probs * (d_prob - jnp.sum(probs * d_prob, axis=-1, keepdims=True))).astype(
            jnp.bfloat16
        )
        d_query_parts.append(
            (
                jnp.einsum("rhqk,rkhd->rqhd", d_scores, k_heads, preferred_element_type=jnp.float32)
                * factor
            ).astype(jnp.bfloat16)
        )
        d_keys = d_keys + jnp.einsum(
            "rhqk,rqhd->rkhd", d_scores, q_block, preferred_element_type=jnp.float32
        )
        d_values = d_values + jnp.einsum(
            "rhqk,rqhd->rkhd",
            probs.astype(jnp.bfloat16),
            grad_block,
            preferred_element_type=jnp.float32,
        )
    grad_packed = jnp.stack(
        [
            jnp.concatenate(d_query_parts, axis=1),
            (d_keys * factor).astype(jnp.bfloat16),
            d_values.astype(jnp.bfloat16),
        ],
        axis=3,
    )
    returned = lax.all_to_all(
        grad_packed.reshape(row_count, row_len, 1, local_heads * 3 * head_width),
        "head",
        split_axis=1,
        concat_axis=2,
        tiled=True,
    )
    returned = returned.reshape(row_count, span_len, HEADS, 3, head_width)
    rotate_back = jax.vjp(turn_fn, qkv_lin[:, :, :, 0])[1]
    d_lin = jnp.stack(
        [
            rotate_back(returned[:, :, :, 0].astype(jnp.float32))[0],
            rotate_back(returned[:, :, :, 1].astype(jnp.float32))[0],
            returned[:, :, :, 2].astype(jnp.float32),
        ],
        axis=3,
    )
    d_lin = d_lin.astype(jnp.bfloat16).reshape(-1, 3 * model_width)
    d_qkv_w = inner(normed, d_lin)
    d_qkv_b = jnp.sum(d_lin.astype(jnp.float32), axis=0)
    d_normed = through(d_lin, w_qkv)
    dx_one, d_gain_one, d_shift_one = norm_back_one(d_normed)
    grad_tokens = (
        (grad_f32 + dx_one + dx_two).reshape(row_count, span_len, model_width).astype(jnp.bfloat16)
    )
    totals = (
        d_qkv_w,
        d_qkv_b,
        d_out_w,
        d_bias_out,
        d_in_w,
        d_in_b,
        d_down_w,
        d_gain_one,
        d_shift_one,
        d_gain_two,
        d_shift_two,
    )
    summed = lax.psum(
        (
            totals[0],
            totals[1],
            totals[2],
            totals[3],
            totals[4],
            totals[5],
            totals[6],
            totals[7],
            totals[8],
            totals[9],
            totals[10],
        ),
        ("dp", "head"),
    )
    return (
        output,
        grad_tokens,
        summed[0],
        summed[1],
        summed[2],
        summed[3],
        summed[4],
        summed[5],
        summed[6],
        summed[3],
        summed[7],
        summed[8],
        summed[9],
        summed[10],
    )


def solution(mesh):
    placed = (
        P("dp", "head", None),
        P("dp", None),
        P(),
        P(),
        P(),
        P(),
        P(),
        P(),
        P(),
        P(),
        P(),
        P(),
        P(),
        P(),
        P("dp", "head", None),
    )
    return jax.shard_map(
        on_device,
        mesh=mesh,
        in_specs=placed,
        out_specs=(
            P("dp", "head", None),
            P("dp", "head", None),
            P(),
            P(),
            P(),
            P(),
            P(),
            P(),
            P(),
            P(),
            P(),
            P(),
            P(),
            P(),
        ),
        check_vma=False,
    )
```

profile of v0, /device:TPU:0, one launch (start us, length us, event | category | flops | bytes accessed | tf_op | source)
XLA Modules:
  0.0 913.0 jit_solution(15552507651041898724)
XLA Ops:
  7.2 3.9 convolution_convert_fusion
  11.1 4.4 reshape.495
  15.5 3.6 copy.108
  19.0 4.5 all-to-all-start.2
  31.4 3.0 fusion.34
  34.4 4.9 convolution_add_fusion
  39.3 8.0 copy.93
  47.3 11.4 %reshape.491 = f32[3,256,12,3,64]{1,0,4,3,2:T(4,128)} reshape(f32[768,2304]{0,1:T(8,128)} %copy.93) | data formatting | bytes 14155776 | tf_op jit(solution)/shard_map/reshape | solution.py:91
  58.8 3.9 slice_bitcast_fusion.1
  67.7 3.6 slice.196
  76.9 3.9 pad_maximum_fusion
  83.3 6.6 fusion.88
  89.9 4.7 all-to-all-start
  94.7 29.7 %convert_reduce_fusion = (f32[3072]{0:T(1024)}, bf16[768,3072]{1,0:T(8,128)(2,1)}, f32[768,3072]{1,0:T(8,128)}) fusion(f32[768,3072]{1,0:T(8,128)} %fusion.88, f32[3072]{0:T(1024)S(1)} %convert_element_type.214, bf16[768,768]{1,0:T(8,128)(2,1)} %bitcast.197, bf16[3072,768]{1,0:T(8,128)(2,1)} %param.23), kind=kOutput, calls=%fused_computation.21 | convolution fusion | flops 3800822784 | bytes 29515776 | tf_op jit(solution)/shard_map/dot_general | solution.py:46
  125.2 3.6 compare_and_fusion.1
  128.7 3.2 copy.109
  131.9 3.4 reshape.496
  136.4 6.5 copy.100
  142.9 7.4 reshape.492
  151.7 10.9 %fusion.87 = (f32[3,3,512]{2,1,0:T(4,128)}, f32[3,3,512,1024]{3,2,1,0:T(8,128)}) fusion(bf16[3,1024,3,3,64]{1,4,3,2,0:T(8,128)(2,1)} %reshape.492, bf16[3,1024,3,64]{1,3,2,0:T(8,128)(2,1)S(1)} %slice_bitcast_fusion.3, pred[3,512,1024]{2,1,0:T(8,128)(4,1)} %get-tuple-element.67), kind=kOutput, calls=%fused_computation.175 | convolution fusion | flops 618130944 | bytes 22235136 | tf_op jit(solution)/shard_map/rqhd,rkhd->rhqk/dot_general | solution.py:112
  162.7 10.0 %fusion = f32[3,3,512]{2,1,0:T(4,128)} fusion(f32[3,3,512,1024]{3,2,1,0:T(8,128)} %get-tuple-element.78, f32[3,3,512]{2,1,0:T(4,128)} %get-tuple-element.77), kind=kLoop, calls=%fused_computation.12 | loop fusion | flops 9432576 | bytes 18911232 | tf_op jit(solution)/shard_map/reduce_sum | solution.py:125
  173.5 12.8 %multiply_reduce_fusion.1 = (f32[3,3,512]{2,1,0:T(4,128)S(1)}, f32[3,3,512,1024]{3,2,1,0:T(8,128)}) fusion(f32[3,3,512,1024]{3,2,1,0:T(8,128)} %get-tuple-element.78, f32[3,3,512]{2,1,0:T(4,128)S(1)} %log_add_fusion.1, bf16[3,1024,3,3,64]{1,4,3,2,0:T(8,128)(2,1)} %reshape.492, bf16[3,1024,3,64]{1,3,2,0:T(8,128)(2,1)} %reshape.496), kind=kOutput, calls=%fused_computation.4 | convolution fusion | flops 618130944 | bytes 39555072 | tf_op jit(solution)/shard_map/rqhd,rkhd->rhqk/dot_general | solution.py:184
  186.3 13.0 %multiply_convert_fusion.1 = bf16[3,3,512,1024]{3,2,1,0:T(8,128)(2,1)S(1)} fusion(f32[3,3,512,1024]{3,2,1,0:T(8,128)} %get-tuple-element.80, f32[3,3,512,1024]{3,2,1,0:T(8,128)} %get-tuple-element.78, f32[3,3,512]{2,1,0:T(4,128)S(1)} %get-tuple-element.79, f32[3,3,512]{2,1,0:T(4,128)S(1)} %log_add_fusion.1), kind=kLoop, calls=%fused_computation.3 | loop fusion | flops 18874368 | bytes 47222784 | tf_op jit(solution)/shard_map/convert_element_type | solution.py:187
  199.4 3.8 fusion.56
  203.2 3.2 fusion.69
  206.3 9.7 %fusion.86 = (f32[3,3,512]{2,1,0:T(4,128)}, f32[3,3,512,1024]{3,2,1,0:T(8,128)}) fusion(bf16[3,1024,3,3,64]{1,4,3,2,0:T(8,128)(2,1)S(1)} %copy-done.4, bf16[3,1024,3,64]{1,3,2,0:T(8,128)(2,1)S(1)} %copy-done.16, pred[3,512,1024]{2,1,0:T(8,128)(4,1)S(1)} %copy-done.23), kind=kOutput, calls=%fused_computation.174 | convolution fusion | flops 618130944 | bytes 22235136 | tf_op jit(solution)/shard_map/rqhd,rkhd->rhqk/dot_general | solution.py:112
  216.0 10.0 %fusion.1 = f32[3,3,512]{2,1,0:T(4,128)} fusion(f32[3,3,512,1024]{3,2,1,0:T(8,128)} %get-tuple-element.76, f32[3,3,512]{2,1,0:T(4,128)} %get-tuple-element.75), kind=kLoop, calls=%fused_computation.13 | loop fusion | flops 9432576 | bytes 18911232 | tf_op jit(solution)/shard_map/reduce_sum | solution.py:125
  226.8 12.8 %multiply_reduce_fusion = (f32[3,3,512]{2,1,0:T(4,128)S(1)}, f32[3,3,512,1024]{3,2,1,0:T(8,128)}) fusion(f32[3,3,512,1024]{3,2,1,0:T(8,128)} %get-tuple-element.76, f32[3,3,512]{2,1,0:T(4,128)S(1)} %log_add_fusion, bf16[3,1024,3,3,64]{1,4,3,2,0:T(8,128)(2,1)} %reshape.492, bf16[3,1024,3,64]{1,3,2,0:T(8,128)(2,1)} %reshape.496), kind=kOutput, calls=%fused_computation.1 | convolution fusion | flops 618130944 | bytes 39555072 | tf_op jit(solution)/shard_map/rqhd,rkhd->rhqk/dot_general | solution.py:184
  239.6 8.8 fusion.5
  248.5 9.1 fusion.52
  257.6 9.1 fusion.51
  266.7 13.0 %multiply_convert_fusion = bf16[3,3,512,1024]{3,2,1,0:T(8,128)(2,1)S(1)} fusion(f32[3,3,512,1024]{3,2,1,0:T(8,128)} %get-tuple-element.82, f32[3,3,512,1024]{3,2,1,0:T(8,128)} %get-tuple-element.76, f32[3,3,512]{2,1,0:T(4,128)S(1)} %get-tuple-element.81, f32[3,3,512]{2,1,0:T(4,128)S(1)} %log_add_fusion), kind=kLoop, calls=%fused_computation | loop fusion | flops 18874368 | bytes 47222784 | tf_op jit(solution)/shard_map/convert_element_type | solution.py:187
  279.7 3.6 copy-done.1
  283.4 3.8 fusion.55
  287.2 9.4 %fusion.48 = bf16[3,1024,3,1,64]{1,4,2,0,3:T(8,128)(2,1)} fusion(f32[3,3,64,1024]{3,2,1,0:T(8,128)S(1)} %fusion.5, f32[3,3,512,1024]{3,2,1,0:T(8,128)} %get-tuple-element.78, f32[3,3,512]{2,1,0:T(4,128)S(1)} %copy-done.31, bf16[3,1024,3,64]{1,3,2,0:T(8,128)(2,1)S(1)} %copy-done.9), kind=kOutput, calls=%fused_computation.103 | convolution fusion | flops 614596608 | bytes 23027712 | tf_op jit(solution)/shard_map/rhqk,rqhd->rkhd/dot_general | solution.py:199
  301.1 4.4 pad_maximum_fusion.2
  305.5 4.4 all-to-all-start.1
  312.0 5.8 fusion.47
  320.4 8.6 copy.111
  329.0 6.8 all-to-all-done.1
  335.8 5.1 all-to-all-start.3
  340.9 11.0 %multiply_convert_fusion.2 = bf16[768,3072]{1,0:T(8,128)(2,1)} fusion(f32[768,3072]{1,0:T(8,128)} %get-tuple-element.39, f32[768,3072]{1,0:T(8,128)} %fusion.88, f32[3072]{0:T(1024)} %copy-done.47), kind=kLoop, calls=%fused_computation.26 | loop fusion | flops 9437184 | bytes 23605248 | tf_op jit(solution)/shard_map/convert_element_type | solution.py:148
  352.0 2.8 fusion.32
  354.7 10.4 %fusion.94 = f32[3072,768]{1,0:T(8,128)} fusion(bf16[768,3072]{1,0:T(8,128)(2,1)} %multiply_convert_fusion.2, bf16[768,768]{1,0:T(8,128)(2,1)} %bitcast.198), kind=kOutput, calls=%fused_computation.182 | convolution fusion | flops 3623878656 | bytes 15335424 | tf_op jit(solution)/shard_map/dot_general | solution.py:40
  365.2 9.0 fusion.93
  374.2 4.3 copy.123
  378.4 4.1 copy.107
  382.5 4.0 reshape.493
  386.6 4.1 fusion.92
  390.7 9.6 %all-to-all-done.3 = bf16[3,1024,1,576]{3,0,2,1:T(4,128)(2,1)} async-done(((bf16[3,1024,1,576]{3,0,2,1:T(4,128)(2,1)}), bf16[3,1024,1,576]{3,0,2,1:T(4,128)(2,1)}, u32[]{:S(2)}, u32[]{:S(2)}) %all-to-all-start.3) | async-done | bytes 3538976 | tf_op jit(solution)/shard_map/all_to_all | solution.py:213
  400.3 9.0 copy.124
  419.9 18.1 %convert_reduce_fusion.1 = (f32[12,3,64]{2,0,1:T(8,128)}, bf16[3,256,12,3,64]{1,0,4,2,3:T(4,128)(2,1)S(1)}) fusion(bf16[3,256,12,1,64]{1,0,4,2,3:T(4,128)(2,1)S(1)} %copy.141, bf16[3,256,12,1,64]{1,0,4,2,3:T(4,128)(2,1)S(1)} %add_bitcast_fusion, bf16[3,256,12,1,64]{1,0,4,2,3:T(4,128)(2,1)S(1)} %add_bitcast_fusion.1), kind=kLoop, calls=%fused_computation.22 | loop fusion | flops 7075584 | bytes 7087104 | tf_op jit(solution)/shard_map/reduce_sum | solution.py:232
  438.1 3.0 copy.117
  443.8 5.0 fusion.91
  451.6 9.0 fusion.90
  460.7 7.6 fusion.89
  472.6 7.5 fusion.80
  480.2 2.8 fusion.38
  483.0 43.7 %all-reduce.8 = (f32[2304]{0:T(1024)}, f32[768]{0:T(1024)}, f32[3072]{0:T(1024)}, f32[768]{0:T(1024)}, f32[768]{0:T(1024)}, /*index=5*/f32[768]{0:T(1024)}, f32[768]{0:T(1024)}) all-reduce(f32[2304]{0:T(1024)} %reduce_sum.170, f32[768]{0:T(1024)} %convert_reduce_fusion.3, ...), channel_id=1, replica_groups=mesh['dp'=8,'head'=4] {'dp','head'}, use_global_device_ids=true, to_apply=%region_14.15 | all-reduce | flops 9216 | bytes 73728 | tf_op jit(solution)/shard_map/psum | solution.py:251
  528.0 5.5 add_convert_fusion.1
  533.5 350.1 %all-reduce.12.cloned.1.call-done = (f32[768,2304]{1,0:T(8,128)}, f32[768,768]{1,0:T(8,128)}, f32[768,3072]{1,0:T(8,128)}, f32[3072,768]{1,0:T(8,128)}) async-done(((f32[768,2304]{1,0:T(8,128)}, f32[768,768]{1,0:T(8,128)}, f32[768,3072]{1,0:T(8,128)}, f32[3072,768]{1,0:T(8,128)}), (f32[768,2304]{1,0:T(8,128)}, f32[768,768]{1,0:T(8,128)}, f32[768,3072]{1,0:T(8,128)}, ...) | async-done | bytes 28311568 | tf_op jit(solution)/shard_map/psum | solution.py:251
  884.8 6.6 copy.148
  892.8 9.3 %copy.150 = f32[768,3072]{1,0:T(8,128)} copy(f32[768,3072]{1,0:T(8,128)} %get-tuple-element.122) | data formatting | bytes 18874368
  902.1 3.7 copy.151
  (208 shorter events, 59.2 us)
Async XLA Ops:
  7.2 27.2 %copy-start = (bf16[768,2304]{1,0:T(8,128)(2,1)S(1)}, bf16[768,2304]{1,0:T(8,128)(2,1)}, u32[]{:S(2)}) copy-start(bf16[768,2304]{1,0:T(8,128)(2,1)} %param.17) | copy-start | bytes 10616836
  19.0 70.9 %all-to-all-start.2 = ((bf16[3,256,4,192]{1,3,0,2:T(8,128)(2,1)}), bf16[3,256,4,192]{1,3,0,2:T(8,128)(2,1)}, u32[]{:S(2)}, u32[]{:S(2)}) async-start(bf16[3,256,4,192]{1,3,0,2:T(8,128)(2,1)} %copy.108), calls=%async_computation.2 | async-start | bytes 2359296 | tf_op jit(solution)/shard_map/all_to_all | solution.py:169
  25.0 14.3 %copy-start.39 = (f32[3,256]{1,0:T(4,128)}, f32[3,256]{1,0:T(4,128)S(1)}, u32[]{:S(2)}) copy-start(f32[3,256]{1,0:T(4,128)S(1)} %broadcast_multiply_fusion.1) | copy-start | bytes 9220
  26.8 12.5 %copy-start.41 = (f32[768]{0:T(1024)}, f32[768]{0:T(1024)S(1)}, u32[]{:S(2)}) copy-start(f32[768]{0:T(1024)S(1)} %div.58) | copy-start | bytes 9220
  27.9 11.4 %copy-start.50 = (f32[768]{0:T(1024)}, f32[768]{0:T(1024)S(1)}, u32[]{:S(2)}) copy-start(f32[768]{0:T(1024)S(1)} %add.180) | copy-start | bytes 9220
  27.9 6.4 copy-start.43
  28.6 2.8 copy-start.32
  29.3 5.1 copy-start.45
  30.0 4.4 copy-start.48
  62.7 5.0 copy-start.7
  62.7 5.0 copy-start.8
  66.2 5.1 copy-start.55
  66.2 5.4 copy-start.61
  71.5 4.4 copy-start.57
  71.5 3.3 copy-start.17
  72.2 2.6 copy-start.26
  72.2 2.6 copy-start.28
  72.2 3.7 copy-start.18
  75.9 7.4 slice-start.4
  76.9 6.3 slice-start.5
  80.8 2.4 copy-start.19
  83.2 11.4 %copy-start.47 = (f32[3072]{0:T(1024)}, f32[3072]{0:T(1024)S(1)}, u32[]{:S(2)}) copy-start(f32[3072]{0:T(1024)S(1)} %convert_element_type.214) | copy-start | bytes 36868
  89.9 46.5 %all-to-all-start = ((bf16[3,256,4,576]{1,3,0,2:T(8,128)(2,1)}), bf16[3,256,4,576]{1,3,0,2:T(8,128)(2,1)}, u32[]{:S(2)}, u32[]{:S(2)}) async-start(bf16[3,256,4,576]{1,3,0,2:T(8,128)(2,1)} %copy.99), calls=%async_computation | async-start | bytes 7077888 | tf_op jit(solution)/shard_map/all_to_all | solution.py:102
  94.7 29.8 %copy-start.58 = (s32[3]{0:T(128)S(1)}, s32[3]{0:T(128)}, u32[]{:S(2)}) copy-start(s32[3]{0:T(128)} %copy-done.57) | copy-start | bytes 40
  151.7 10.9 %copy-start.15 = (bf16[3,1024,3,64]{1,3,2,0:T(8,128)(2,1)}, bf16[3,1024,3,64]{1,3,2,0:T(8,128)(2,1)S(1)}, u32[]{:S(2)}) copy-start(bf16[3,1024,3,64]{1,3,2,0:T(8,128)(2,1)S(1)} %slice_bitcast_fusion.3) | copy-start | bytes 3538948
  173.5 12.8 %copy-start.30 = (f32[3,3,512]{2,1,0:T(4,128)}, f32[3,3,512]{2,1,0:T(4,128)S(1)}, u32[]{:S(2)}) copy-start(f32[3,3,512]{2,1,0:T(4,128)S(1)} %log_add_fusion.1) | copy-start | bytes 55300
  186.3 13.0 %copy-start.4 = (bf16[3,1024,3,3,64]{1,4,3,2,0:T(8,128)(2,1)S(1)}, bf16[3,1024,3,3,64]{1,4,3,2,0:T(8,128)(2,1)}, u32[]{:S(2)}) copy-start(bf16[3,1024,3,3,64]{1,4,3,2,0:T(8,128)(2,1)} %reshape.492) | copy-start | bytes 10616836
  199.3 3.8 copy-start.16
  203.2 3.2 copy-start.23
  226.8 12.8 %copy-start.9 = (bf16[3,1024,3,64]{1,3,2,0:T(8,128)(2,1)S(1)}, bf16[3,1024,3,64]{1,3,2,0:T(8,128)(2,1)}, u32[]{:S(2)}) copy-start(bf16[3,1024,3,64]{1,3,2,0:T(8,128)(2,1)} %reshape.496) | copy-start | bytes 3538948
  239.6 8.8 copy-start.5
  239.6 8.8 copy-start.35
  239.6 8.8 copy-start.36
  248.5 9.1 copy-start.37
  248.5 9.1 copy-start.38
  279.7 3.6 copy-start.1
  283.3 3.8 copy-start.31
  305.5 30.2 %all-to-all-start.1 = ((bf16[3,1024,1,192]{3,0,2,1:T(4,128)(2,1)}), bf16[3,1024,1,192]{3,0,2,1:T(4,128)(2,1)}, u32[]{:S(2)}, u32[]{:S(2)}) async-start(bf16[3,1024,1,192]{3,0,2,1:T(4,128)(2,1)} %pad_maximum_fusion.2), calls=%async_computation.1 | async-start | bytes 4194304 | tf_op jit(solution)/shard_map/all_to_all | solution.py:133
  312.0 5.8 copy-start.14
  335.8 64.5 %all-to-all-start.3 = ((bf16[3,1024,1,576]{3,0,2,1:T(4,128)(2,1)}), bf16[3,1024,1,576]{3,0,2,1:T(4,128)(2,1)}, u32[]{:S(2)}, u32[]{:S(2)}) async-start(bf16[3,1024,1,576]{3,0,2,1:T(4,128)(2,1)} %copy.111), calls=%async_computation.3 | async-start | bytes 10485760 | tf_op jit(solution)/shard_map/all_to_all | solution.py:213
  340.8 542.7 %all-reduce.12.cloned.1.call-start = ((), (), s32[]{:S(2)}) async-start(), calls=%async_computation.4 | async-start | bytes 56623104 | tf_op jit(solution)/shard_map/psum | solution.py:251
  340.9 11.1 %copy-start.33 = (f32[768]{0:T(1024)S(1)}, f32[768]{0:T(1024)}, u32[]{:S(2)}) copy-start(f32[768]{0:T(1024)} %copy-done.32) | copy-start | bytes 9220
  340.9 11.0 %copy-start.40 = (f32[3,256]{1,0:T(4,128)S(1)}, f32[3,256]{1,0:T(4,128)}, u32[]{:S(2)}) copy-start(f32[3,256]{1,0:T(4,128)} %copy-done.39) | copy-start | bytes 9220
  340.9 11.0 %copy-start.49 = (f32[768]{0:T(1024)S(1)}, f32[768]{0:T(1024)}, u32[]{:S(2)}) copy-start(f32[768]{0:T(1024)} %copy-done.48) | copy-start | bytes 9220
  340.9 11.0 %copy-start.54 = (f32[3,256]{1,0:T(4,128)S(1)}, f32[3,256]{1,0:T(4,128)}, u32[]{:S(2)}) copy-start(f32[3,256]{1,0:T(4,128)} %get-tuple-element.71) | copy-start | bytes 9220
  354.7 10.4 %copy-start.20 = (bf16[768,768]{1,0:T(8,128)(2,1)S(1)}, bf16[768,768]{1,0:T(8,128)(2,1)}, u32[]{:S(2)}) copy-start(bf16[768,768]{1,0:T(8,128)(2,1)} %get-tuple-element.52) | copy-start | bytes 3538948
  413.2 3.8 copy-start.6
  441.0 2.8 copy-start.24
  460.7 7.6 copy-start.2
  460.7 7.6 copy-start.25
  460.7 7.6 copy-start.62
  468.3 4.3 copy-start.42
  468.3 4.3 copy-start.46
  472.6 7.6 copy-start.51
  472.6 7.6 copy-start.3
  472.6 7.6 copy-start.11
  472.6 7.6 copy-start.44
  480.2 2.8 copy-start.12
  480.2 2.8 copy-start.52
  480.2 2.8 copy-start.53
  884.8 6.6 copy-start.22
  891.4 10.7 %slice-start.1 = ((s8[9437184]{0:T(1024)(128)(4,1)}), s8[4194304]{0:T(1024)(128)(4,1)S(1)}, s32[]{:S(2)}) async-start(s8[9437184]{0:T(1024)(128)(4,1)} %bitcast.193), calls=%async_computation.6 | async-start | bytes 8388608
  892.8 9.3 %slice-start.2 = ((s8[9437184]{0:T(1024)(128)(4,1)}), s8[4194304]{0:T(1024)(128)(4,1)S(1)}, s32[]{:S(2)}) async-start(s8[9437184]{0:T(1024)(128)(4,1)} %bitcast.193), calls=%async_computation.7 | async-start | bytes 8388608
  892.8 9.3 %slice-start.3 = ((s8[9437184]{0:T(1024)(128)(4,1)}), s8[1048576]{0:T(1024)(128)(4,1)S(1)}, s32[]{:S(2)}) async-start(s8[9437184]{0:T(1024)(128)(4,1)} %bitcast.193), calls=%async_computation.8 | async-start | bytes 2097152
  (10 other events, 15.9 us)
Sparse Core Ops, SparseCore 0:
  449.0 434.4 all-reduce.11
where the time goes:
time: 919 us; the launch traced here: 913 us
  waiting for transfers between devices  368 us (40%)
  matrix products  199 us (22%)
  local copies, waits for them, and re-layouts  140 us (15%)
  other arithmetic  128 us (14%)
  blocking collectives  43.7 us (5%)
  starting transfers between devices  18.8 us (2%)
  between operations  15.2 us (2%)
    psum x1, waiting for transfers between devices, on_device(): lax.psum((totals[0], totals[1], totals[2], totals[3], totals[4], totals[5...  350 us
    dot_general x4, matrix products, through(): lax.dot_general(left_mat, right_mat, (((1,), (1,)), ((), ())), preferred_...  50.2 us
    psum x1, blocking collectives, on_device(): lax.psum((totals[0], totals[1], totals[2], totals[3], totals[4], totals[5...  43.7 us
    unnamed x143, local copies, waits for them, and re-layouts  31.6 us
    dot_general x4, matrix products, inner(): lax.dot_general(left_mat, right_mat, (((0,), (0,)), ((), ())), preferred_...  28.6 us
    convert_element_type x2, other arithmetic, on_device(): (probs * (d_prob - jnp.sum(probs * d_prob, axis=-1, keepdims=True))).asty...  26 us
    dot_general x2, matrix products, on_device(): jnp.einsum('rqhd,rkhd->rhqk', grad_block, v_heads, preferred_element_type...  25.6 us
    dot_general x2, matrix products, scored(): jnp.einsum('rqhd,rkhd->rhqk', q_block, k_heads, preferred_element_type=jn...  20.6 us
  transfers between devices with their start and end apart: 5, of which 4 were waited for; matrix products, arithmetic and copies ran while one was open for 24% of the time, Pallas kernels for 0%

commit v1 on v0

v1 whole, which is shorter than its diff:
```python
import math, functools
import jax
import jax.numpy as jnp
from jax import lax
from jax.experimental import pallas as pl
from jax.experimental.pallas import tpu as pltpu

bf = jnp.bfloat16
f32 = jnp.float32
NN = (((1,), (0,)), ((), ()))
NT = (((1,), (1,)), ((), ()))
TN = (((0,), (0,)), ((), ()))


def mm(a, b, dims=NN):
    return lax.dot_general(a, b, dims, preferred_element_type=f32)


def norm_parts(x):
    center = x - jnp.mean(x, axis=-1, keepdims=True)
    rho = lax.rsqrt(jnp.mean(center * center, axis=-1, keepdims=True) + 1e-5)
    return center * rho, rho


def normal_cdf(x):
    bell = jnp.exp(-0.5 * x * x)
    t = 1.0 / (1.0 + (0.3275911 * math.sqrt(0.5)) * jnp.abs(x))
    poly = t * (0.127414796 + t * (-0.142248368 + t * (0.7107068705 + t * (-0.7265760135 + t * 0.5307027145))))
    tail = poly * bell
    return jnp.where(x >= 0, 1.0 - tail, tail), bell


def mlp_body(core_ref, x_ref, g_ref, wi_ref, wd_ref, bi_ref, gain_ref, bias_ref,
             out_ref, e_ref, gwi_ref, gwd_ref, gbi_ref, ln_ref,
             h_s, ht_s, gt_s, out_s, dh_s, gwi_s, gwd_s):
    j, i = pl.program_id(0), pl.program_id(1)
    nj, ni = pl.num_programs(0), pl.num_programs(1)
    gain = gain_ref[...].astype(f32)

    @pl.when(j == 0)
    def _():
        n, _ = norm_parts(x_ref[...].astype(f32))
        h = (n * gain + bias_ref[...].astype(f32)).astype(bf)
        h_s[i] = h
        ht_s[i] = h.T
        gt_s[i] = g_ref[...].T

    h = h_s[i]
    pre = mm(h, wi_ref[...]) + bi_ref[...].astype(f32)
    cdf, bell = normal_cdf(pre)
    act = (pre * cdf).astype(bf)
    slope = cdf + pre * bell * (1.0 / math.sqrt(2.0 * math.pi))
    d_act = mm(g_ref[...], wd_ref[...], NT)
    d_pre32 = d_act * slope
    d_pre = d_pre32.astype(bf)
    out = mm(act, wd_ref[...])
    dh = mm(d_pre, wi_ref[...], NT)
    gwi = mm(ht_s[i], d_pre)
    gwd = mm(gt_s[i], act)
    gbi = jnp.sum(d_pre.astype(f32), axis=0, keepdims=True)

    @pl.when(i == 0)
    def _():
        gwi_s[...] = gwi
        gwd_s[...] = gwd
        gbi_ref[...] = gbi

    @pl.when(i > 0)
    def _():
        gwi_s[...] += gwi
        gwd_s[...] += gwd
        gbi_ref[...] += gbi

    @pl.when(j == 0)
    def _():
        out_s[i] = out
        dh_s[i] = dh

    @pl.when(j > 0)
    def _():
        out_s[i] += out
        dh_s[i] += dh

    @pl.when(i == ni - 1)
    def _():
        gwi_ref[0] = gwi_s[...].astype(bf)
        gwd_ref[...] = gwd_s[...].astype(bf).T

    @pl.when(jnp.logical_and(j == nj - 1, i == 0))
    def _():
        ln_ref[...] = jnp.zeros_like(ln_ref)

    @pl.when(j == nj - 1)
    def _():
        d = dh_s[i]
        n, _ = norm_parts(x_ref[...].astype(f32))
        out_ref[...] = out_s[i].astype(bf)
        e_ref[...] = (d * gain).astype(bf)
        ln_ref[0:1, :] += jnp.sum(d * n, axis=0, keepdims=True)
        ln_ref[1:2, :] += jnp.sum(d, axis=0, keepdims=True)


def mlp(core, x, g, w_in, w_down, b_in, gain, bias, parts=2, tile=512, fft=768):
    toks, d = x.shape
    ff = w_in.shape[1] // parts
    nj, ni = ff // fft, toks // tile
    row = lambda v: v.reshape(1, -1)
    spec = pl.BlockSpec
    last = lambda j, i, c: (jnp.where(j == nj - 1, i, 0), 0)
    return pl.pallas_call(
        mlp_body,
        out_shape=(
            jax.ShapeDtypeStruct((toks, d), bf),
            jax.ShapeDtypeStruct((toks, d), bf),
            jax.ShapeDtypeStruct((nj, d, fft), bf),
            jax.ShapeDtypeStruct((ff, d), bf),
            jax.ShapeDtypeStruct((1, ff), f32),
            jax.ShapeDtypeStruct((8, d), f32),
        ),
        grid_spec=pltpu.PrefetchScalarGridSpec(
            num_scalar_prefetch=1,
            grid=(nj, ni),
            in_specs=[
                spec((tile, d), lambda j, i, c: (i, 0)),
                spec((tile, d), lambda j, i, c: (i, 0)),
                spec((d, fft), lambda j, i, c: (0, c[0] * nj + j)),
                spec((fft, d), lambda j, i, c: (c[0] * nj + j, 0)),
                spec((1, fft), lambda j, i, c: (0, c[0] * nj + j)),
                spec((1, d), lambda j, i, c: (0, 0)),
                spec((1, d), lambda j, i, c: (0, 0)),
            ],
            out_specs=[
                spec((tile, d), last),
                spec((tile, d), last),
                spec((1, d, fft), lambda j, i, c: (j, 0, 0)),
                spec((fft, d), lambda j, i, c: (j, 0)),
                spec((1, fft), lambda j, i, c: (0, j)),
                spec((8, d), lambda j, i, c: (0, 0)),
            ],
            scratch_shapes=[
                pltpu.VMEM((ni, tile, d), bf),
                pltpu.VMEM((ni, d, tile), bf),
                pltpu.VMEM((ni, d, tile), bf),
                pltpu.VMEM((ni, tile, d), f32),
                pltpu.VMEM((ni, tile, d), f32),
                pltpu.VMEM((d, fft), f32),
                pltpu.VMEM((d, fft), f32),
            ],
        ),
        compiler_params=pltpu.CompilerParams(vmem_limit_bytes=56 * 2**20),
        cost_estimate=pl.CostEstimate(flops=12 * toks * d * ff, bytes_accessed=30 * 2**20, transcendentals=toks * ff),
        name="mlp",
    )(core, x, g, w_in, w_down, row(b_in), row(gain), row(bias))


HW = 64
ROT = 16


def rope(u, cos, sin, back):
    t, width = u.shape
    lane = lax.broadcasted_iota(jnp.int32, (t, 128), 1)
    inner = lane % HW
    low = inner < ROT // 2
    outs = []
    for b in range(width // 128):
        v = u[:, b * 128:(b + 1) * 128]
        lo_rot, hi_rot = (2 * b) % 3 != 2, (2 * b + 1) % 3 != 2
        if (2 * b + 1) * HW >= 9 * HW:
            hi_rot = False
        if not (lo_rot or hi_rot):
            outs.append(v)
            continue
        turned = inner < ROT
        if not hi_rot:
            turned = turned & (lane < HW)
        if not lo_rot:
            turned = turned & (lane >= HW)
        up = pltpu.roll(v, 128 - ROT // 2, 1)
        down = pltpu.roll(v, ROT // 2, 1)
        if back:
            swapped = jnp.where(low, up, -down)
        else:
            swapped = jnp.where(low, -up, down)
        outs.append(jnp.where(turned, v * cos + swapped * sin, v))
    return jnp.concatenate(outs, axis=1)


def attn_body(x_ref, do_ref, w_ref, b_ref, gain_ref, bias_ref, cos_ref, sin_ref, start_ref,
              ctx_ref, e_ref, gw_ref, gb_ref, ln_ref,
              nb_s, n_s, q_s, k_s, v_s, do_s, o_s, dq_s, dk_s, dv_s, gw_s):
    r = pl.program_id(0)
    nr = pl.num_programs(0)
    row_len = x_ref.shape[1]
    nh = q_s.shape[0]
    ch = 256
    nch = row_len // ch
    gain = gain_ref[...].astype(f32)
    bias = bias_ref[...].astype(f32)

    @pl.when(r == 0)
    def _():
        gw_s[...] = jnp.zeros_like(gw_s)
        gb_ref[...] = jnp.zeros_like(gb_ref)
        ln_ref[...] = jnp.zeros_like(ln_ref)

    def project(ci, _):
        rows = pl.ds(pl.multiple_of(ci * ch, ch), ch)
        n, _ = norm_parts(x_ref[0, rows, :].astype(f32))
        n_s[rows, :] = n
        normed = (n * gain + bias).astype(bf)
        nb_s[rows, :] = normed
        lin = mm(normed, w_ref[...]) + b_ref[...].astype(f32)
        lin = rope(lin, cos_ref[0, rows, :], sin_ref[0, rows, :], False)
        for h in range(nh):
            q_s[h, rows, :] = (lin[:, h * 192:h * 192 + 64].astype(bf) * bf(0.125))
            k_s[h, rows, :] = lin[:, h * 192 + 64:h * 192 + 128].astype(bf)
            v_s[h, rows, :] = lin[:, h * 192 + 128:h * 192 + 192].astype(bf)
            do_s[h, rows, :] = do_ref[0, rows, h * 64:h * 64 + 64]
        return 0

    lax.fori_loop(0, nch, project, 0)

    def head(h, _):
        kt = k_s[h].T
        vt = v_s[h].T
        dot_ = do_s[h].astype(f32).T
        for qb in range(nch):
            kn = (qb + 1) * ch
            qs = slice(qb * ch, kn)
            q = q_s[h, qs, :]
            do = do_s[h, qs, :]
            st = mm(k_s[h, 0:kn, :], q, NT)
            kpos = lax.broadcasted_iota(jnp.int32, (kn, ch), 0)
            first = start_ref[0, :, qs]
            keep = kpos >= first
            qpos = lax.broadcasted_iota(jnp.int32, (kn, ch), 1) + qb * ch
            keep = keep & (kpos <= qpos)
            st = jnp.where(keep, st, -1e9)
            top = jnp.max(st, axis=0, keepdims=True)
            p = jnp.exp(st - top)
            p = p * (1.0 / jnp.sum(p, axis=0, keepdims=True))
            pb = p.astype(bf)
            ot = mm(vt[:, 0:kn], pb)
            delta = jnp.sum(ot * dot_[:, qs], axis=0, keepdims=True)
            dpt = mm(v_s[h, 0:kn, :], do, NT)
            ds = (p * (dpt - delta)).astype(bf)
            o_s[h, qs, :] = ot.T
            dq_s[h, qs, :] = mm(kt[:, 0:kn], ds).T * 0.125
            dv = mm(pb, do)
            dk = mm(ds, q)
            if qb:
                dv_s[h, 0:qb * ch, :] += dv[0:qb * ch]
                dk_s[h, 0:qb * ch, :] += dk[0:qb * ch]
            dv_s[h, qs, :] = dv[qb * ch:]
            dk_s[h, qs, :] = dk[qb * ch:]
        return 0

    lax.fori_loop(0, nh, head, 0)

    def back(ci, _):
        rows = pl.ds(pl.multiple_of(ci * ch, ch), ch)
        parts = []
        for h in range(nh):
            parts += [dq_s[h, rows, :], dk_s[h, rows, :], dv_s[h, rows, :]]
        parts.append(jnp.zeros((ch, 64), f32))
        d = jnp.concatenate(parts, axis=1).astype(bf).astype(f32)
        d = rope(d, cos_ref[0, rows, :], sin_ref[0, rows, :], True).astype(bf)
        gb_ref[...] += jnp.sum(d.astype(f32), axis=0, keepdims=True)
        dn = mm(d, w_ref[...], NT)
        n = n_s[rows, :]
        ln_ref[0:1, :] += jnp.sum(dn * n, axis=0, keepdims=True)
        ln_ref[1:2, :] += jnp.sum(dn, axis=0, keepdims=True)
        e_ref[0, rows, :] = (dn * gain).astype(bf)
        gw_s[...] += mm(d.T, nb_s[rows, :])
        ctx_ref[0, rows, :] = jnp.concatenate([o_s[h, rows, :] for h in range(nh)], axis=1).astype(bf)
        return 0

    lax.fori_loop(0, nch, back, 0)

    @pl.when(r == nr - 1)
    def _():
        gw_ref[...] = gw_s[0:gw_ref.shape[0], :].astype(bf)


def attention(x, do, w, b, gain, bias, cos, sin, start):
    rows, row_len, d = x.shape
    width = w.shape[1]
    nh = do.shape[2] // HW
    row = lambda v: v.reshape(1, -1)
    spec = pl.BlockSpec
    per_row = lambda *s: spec((1,) + s, lambda r: (r, 0, 0))
    whole = lambda *s: spec(s, lambda r: (0, 0))
    real = nh * 3 * HW
    return pl.pallas_call(
        attn_body,
        grid=(rows,),
        out_shape=(
            jax.ShapeDtypeStruct((rows, row_len, nh * HW), bf),
            jax.ShapeDtypeStruct((rows, row_len, d), bf),
            jax.ShapeDtypeStruct((real, d), bf),
            jax.ShapeDtypeStruct((1, width), f32),
            jax.ShapeDtypeStruct((8, d), f32),
        ),
        in_specs=[
            per_row(row_len, d), per_row(row_len, nh * HW), whole(d, width), whole(1, width),
            whole(1, d), whole(1, d), per_row(row_len, 128), per_row(row_len, 128), per_row(1, row_len),
        ],
        out_specs=[
            per_row(row_len, nh * HW), per_row(row_len, d), whole(real, d), whole(1, width), whole(8, d),
        ],
        scratch_shapes=[
            pltpu.VMEM((row_len, d), bf),
            pltpu.VMEM((row_len, d), f32),
            pltpu.VMEM((nh, row_len, HW), bf),
            pltpu.VMEM((nh, row_len, HW), bf),
            pltpu.VMEM((nh, row_len, HW), bf),
            pltpu.VMEM((nh, row_len, HW), bf),
            pltpu.VMEM((nh, row_len, HW), f32),
            pltpu.VMEM((nh, row_len, HW), f32),
            pltpu.VMEM((nh, row_len, HW), f32),
            pltpu.VMEM((nh, row_len, HW), f32),
            pltpu.VMEM((width, d), f32),
        ],
        compiler_params=pltpu.CompilerParams(vmem_limit_bytes=56 * 2**20),
        cost_estimate=pl.CostEstimate(flops=rows * row_len * (6 * d * real + 6 * row_len * nh * HW * 4), bytes_accessed=20 * 2**20, transcendentals=rows * nh * row_len * row_len // 2),
        name="attention",
    )(x, do, w, row(b), row(gain), row(bias), cos, sin, start)


from jax.sharding import PartitionSpec as P

HEADS = 12


def swap(x, axis, bit):
    n = lax.axis_size(axis)
    return lax.ppermute(x, axis, [(i, i ^ bit) for i in range(n)])


def pair(mine, other, bit, dim):
    first = jnp.where(bit == 0, mine, other)
    second = jnp.where(bit == 0, other, mine)
    return jnp.concatenate([first, second], axis=dim)


def rs_step(parts, axis, bit, mine):
    keep = lax.dynamic_index_in_dim(parts, mine, 0, False)
    send = lax.dynamic_index_in_dim(parts, 1 - mine, 0, False)
    return (keep.astype(f32) + swap(send, axis, bit).astype(f32)).astype(bf)


def rs_cross(parts, axis, count, step, mine):
    total = lax.dynamic_index_in_dim(parts, mine, 0, False).astype(f32)
    for k in range(1, count):
        total = total + swap(lax.dynamic_index_in_dim(parts, mine ^ k, 0, False), axis, step * k).astype(f32)
    return total.astype(bf)


def ag_step(x, axis, bit):
    return jnp.stack([x, swap(x, axis, bit)])


def ag_cross(x, axis, count, step):
    return jnp.stack([x] + [swap(x, axis, step * k) for k in range(1, count)])


def tables(lengths, row_len):
    pos = jnp.arange(row_len, dtype=jnp.int32)[None, :]
    first_end = lengths[:, 0:1]
    second_end = first_end + lengths[:, 1:2]
    start = jnp.where(pos < first_end, 0, jnp.where(pos < second_end, first_end, second_end))
    half = ROT // 2
    freq = 1.0 / 10000.0 ** (jnp.arange(half, dtype=f32) * 2.0 / ROT)
    angle = (pos - start)[:, None, :].astype(f32) * freq[None, :, None]

    def full(t):
        t = jnp.concatenate([t, t], axis=1)
        t = jnp.pad(t, ((0, 0), (0, HW - ROT), (0, 0)))
        return jnp.swapaxes(jnp.concatenate([t, t], axis=1), 1, 2)

    return full(jnp.cos(angle)), full(jnp.sin(angle)), start[:, None, :]


def fill_body(own_ref, pieces_ref, wi_ref, wd_ref):
    _, nc, ny, nz, nx, rows, d = pieces_ref.shape
    x, c, y, z = own_ref[0], own_ref[1], own_ref[2], own_ref[3]
    for jc in range(nc):
        for jx in range(nx):
            for jy in range(ny):
                for jz in range(nz):
                    at = ((y ^ jy) * nz + (z ^ jz)) * rows
                    block = ((c ^ jc) * nx + (x ^ jx))
                    wi_ref[pl.ds(pl.multiple_of(at, 8), rows), pl.ds(pl.multiple_of(block * d, 128), d)] = pieces_ref[0, jc, jy, jz, jx].astype(f32)
                    wd_ref[pl.ds(pl.multiple_of(block * d + at, 8), rows), :] = pieces_ref[1, jc, jy, jz, jx].astype(f32)


def fill_mlp(own, pieces):
    _, nc, ny, nz, nx, rows, d = pieces.shape
    vm = pl.BlockSpec(memory_space=pltpu.VMEM)
    return pl.pallas_call(
        fill_body,
        out_shape=(jax.ShapeDtypeStruct((d, nc * nx * d), f32), jax.ShapeDtypeStruct((nc * nx * d, d), f32)),
        in_specs=[pl.BlockSpec(memory_space=pltpu.SMEM), vm],
        out_specs=(vm, vm),
        compiler_params=pltpu.CompilerParams(vmem_limit_bytes=56 * 2**20),
        name="fill_mlp",
    )(own, pieces)


def fill_attn_body(own_ref, pieces_ref, wq_ref, wo_ref, s):
    nc, ny, nz, nx, rows, d = pieces_ref.shape
    x, c, y, z = own_ref[0], own_ref[1], own_ref[2], own_ref[3]
    real = wq_ref.shape[1] // (nc * nx)
    out_rows = wo_ref.shape[0] // (nc * nx)
    for jc in range(nc):
        for jx in range(nx):
            block = ((c ^ jc) * nx + (x ^ jx))
            for jy in range(ny):
                for jz in range(nz):
                    at = ((y ^ jy) * nz + (z ^ jz)) * rows
                    s[block, pl.ds(pl.multiple_of(at, 8), rows), :] = pieces_ref[jc, jy, jz, jx].astype(f32)
    for b in range(nc * nx):
        wq_ref[:, b * real:(b + 1) * real] = s[b, 0:real, :].T
        wo_ref[b * out_rows:(b + 1) * out_rows, :] = s[b, real:real + out_rows, :]


def fill_attn(own, pieces, real):
    nc, ny, nz, nx, rows, d = pieces.shape
    vm = pl.BlockSpec(memory_space=pltpu.VMEM)
    return pl.pallas_call(
        fill_attn_body,
        out_shape=(jax.ShapeDtypeStruct((d, nc * nx * real), f32), jax.ShapeDtypeStruct((d, d), f32)),
        in_specs=[pl.BlockSpec(memory_space=pltpu.SMEM), vm],
        out_specs=(vm, vm),
        scratch_shapes=[pltpu.VMEM((nc * nx, d, d), f32)],
        compiler_params=pltpu.CompilerParams(vmem_limit_bytes=56 * 2**20),
        name="fill_attn",
    )(own, pieces)


def on_device(tokens, lengths, w_qkv, b_qkv, w_out, b_out, w_in, b_in, w_down, b_down,
              norm1_gain, norm1_bias, norm2_gain, norm2_bias, cotangent):
    rows, span, d = tokens.shape
    ff = w_in.shape[1]
    head = lax.axis_index("head")
    dp = lax.axis_index("dp")
    x, c = head // 2, head % 2
    y, z = dp % 2, dp // 2
    nz = lax.axis_size("dp") // 2
    own = jnp.stack([x, c, y, z]).astype(jnp.int32)
    row_len = 4 * span
    lh = HEADS // 4
    hd = lh * HW

    tok2 = pair(tokens, swap(tokens, "head", 1), c, 1)
    g2 = pair(cotangent, swap(cotangent, "head", 1), c, 1)
    far = swap(tokens, "head", 2)
    far2 = pair(far, swap(far, "head", 1), c, 1)
    tok4 = pair(tok2, far2, x, 1)

    w_out_c = lax.dynamic_slice_in_dim(w_out, c * 2 * hd, 2 * hd, 0)
    at = (c * 2 + x) * (3 * hd)
    w_q = jnp.pad(lax.dynamic_slice_in_dim(w_qkv, at, 3 * hd, 1), ((0, 0), (0, HW)))
    b_q = jnp.pad(lax.dynamic_slice_in_dim(b_qkv, at, 3 * hd, 0), ((0, HW)))
    cos, sin, start = tables(lengths, row_len)

    g2f = g2.reshape(-1, d)
    dctx = mm(g2f, w_out_c, NT).astype(bf).reshape(rows, 2 * span, 2, hd)
    d_mine = lax.dynamic_index_in_dim(dctx, x, 2, False)
    d_far = swap(lax.dynamic_index_in_dim(dctx, 1 - x, 2, False), "head", 2)
    do4 = pair(d_mine, d_far, x, 1)

    m_out, m_e, gwi, gwd, gbi, ln2 = mlp(c[None], tok2.reshape(-1, d), g2f, w_in, w_down, b_in, norm2_gain, norm2_bias)
    ctx, e1, gq, gbq, ln1 = attention(tok4, do4, w_q, b_q, norm1_gain, norm1_bias, cos, sin, start)

    gm = jnp.stack([gwi, gwd.reshape(2, d, d)])
    gm = gm.reshape(2, 2, 2, nz, d // (2 * nz), d)
    gm = rs_step(jnp.moveaxis(gm, 2, 0), "dp", 1, y)
    gm = rs_cross(jnp.moveaxis(gm, 2, 0), "dp", nz, 2, z)
    gm = rs_step(jnp.moveaxis(gm, 1, 0), "head", 2, x)
    f = ag_step(gm, "head", 2)
    f = ag_cross(f, "dp", nz, 2)
    f = ag_step(f, "dp", 1)
    f = ag_step(f, "head", 1)
    grad_w_in, grad_w_down = fill_mlp(own, jnp.moveaxis(f, 4, 0))

    ctx_h = ctx.reshape(rows, 2, 2 * span, hd)
    c_mine = lax.dynamic_index_in_dim(ctx_h, x, 1, False)
    c_far = swap(lax.dynamic_index_in_dim(ctx_h, 1 - x, 1, False), "head", 2)
    ctx2 = pair(c_mine, c_far, x, 2).reshape(-1, 2 * hd)
    part = (mm(ctx2, w_out_c) + m_out.astype(f32)).astype(bf).reshape(rows, 2, span, d)
    gwo = mm(ctx2, g2f, TN).astype(bf).reshape(2, hd, d)
    total = rs_step(jnp.moveaxis(part, 1, 0), "head", 1, c).astype(f32)
    bias = (b_out.astype(f32) + b_down.astype(f32))
    output = (tokens.astype(f32) + total + bias).astype(bf)

    e1 = e1.reshape(rows, 2, 2, span, d)
    e2 = m_e.reshape(rows, 1, 2, span, d)
    here = (jnp.arange(2) == x).reshape(1, 2, 1, 1, 1)
    e = (e1.astype(f32) + jnp.where(here, e2.astype(f32), 0.0)).astype(bf)
    e = rs_step(jnp.moveaxis(e, 2, 0), "head", 1, c)
    e = rs_step(jnp.moveaxis(e, 1, 0), "head", 2, x).astype(f32)
    n, rho = norm_parts(tokens.astype(f32))
    dx = rho * (e - jnp.mean(e, -1, keepdims=True) - n * jnp.mean(e * n, -1, keepdims=True))
    grad_tokens = (cotangent.astype(f32) + dx).astype(bf)

    gwo = rs_step(gwo, "head", 2, x)
    ga = jnp.concatenate([gq, gwo], axis=0).reshape(2, nz, d // (2 * nz), d)
    ga = rs_step(ga, "dp", 1, y)
    ga = rs_cross(ga, "dp", nz, 2, z)
    f = ag_step(ga, "head", 2)
    f = ag_cross(f, "dp", nz, 2)
    f = ag_step(f, "dp", 1)
    f = ag_step(f, "head", 1)
    grad_w_qkv, grad_w_out = fill_attn(own, f, 3 * hd)

    gsum = jnp.sum(cotangent.astype(f32), axis=(0, 1))
    v_in = lax.dynamic_update_slice(jnp.zeros((ff,), f32), gbi[0], (c * (ff // 2),))
    v_q = lax.dynamic_update_slice(jnp.zeros((3 * d,), f32), gbq[0, :3 * hd], (at,))
    v = jnp.concatenate([v_in, v_q, gsum, ln1[0], ln1[1], ln2[0], ln2[1]]).reshape(-1, 128)
    for axis in ("head", "dp"):
        bit = 1
        while bit < lax.axis_size(axis):
            v = v + swap(v, axis, bit)
            bit *= 2
    v = v.reshape(-1)
    cut = lambda a, n: v[a:a + n]
    o = ff + 3 * d
    return (output, grad_tokens, grad_w_qkv, cut(ff, 3 * d), grad_w_out, cut(o, d), grad_w_in, cut(0, ff),
            grad_w_down, cut(o, d), cut(o + d, d), cut(o + 2 * d, d), cut(o + 3 * d, d), cut(o + 4 * d, d))


def solution(mesh):
    split = P("dp", "head", None)
    return jax.shard_map(
        on_device, mesh=mesh,
        in_specs=(split, P("dp", None)) + (P(),) * 12 + (split,),
        out_specs=(split, split) + (P(),) * 12,
        check_vma=False,
    )
```

time: 919 us -> 478 us (0.52)
  waiting for transfers between devices: 368 us -> 165 us
  matrix products: 199 us -> 5.78 us
  Pallas kernels: 0 us -> 132 us
  local copies, waits for them, and re-layouts: 140 us -> 44.8 us
  other arithmetic: 128 us -> 66.2 us
  blocking collectives: 43.7 us -> 0 us
  starting transfers between devices: 18.8 us -> 53.7 us
  between operations: 15.2 us -> 1.73 us
    psum x1 -> x0, waiting for transfers between devices: 350 us -> none  [on_device(): lax.psum((totals[0], totals[1], totals[2], totals[3], totals[4], totals[5...]
    dot_general x24 -> x3, matrix products: 199 us -> 5.78 us  [mm(): return lax.dot_general(a, b, dims, preferred_element_type=f32)]
    ppermute x0 -> x36, waiting for transfers between devices: none -> 165 us  [swap(): return lax.ppermute(x, axis, [(i, i ^ bit) for i in range(n)])]
    pallas_call x0 -> x4, Pallas kernels: none -> 132 us  [the longest x1 68.5 us: attention(): pl.pallas_call(attn_body, grid=(rows,), out_shape=(jax.ShapeDtypeStruct((...]
    ppermute x0 -> x36, starting transfers between devices: none -> 53.7 us  [swap(): return lax.ppermute(x, axis, [(i, i ^ bit) for i in range(n)])]
    psum x1 -> x0, blocking collectives: 43.7 us -> none  [on_device(): lax.psum((totals[0], totals[1], totals[2], totals[3], totals[4], totals[5...]
    convert_element_type x17 -> x9, other arithmetic: 53.8 us -> 12.3 us  [the longest x5 5.77 us: rs_step(): return (keep.astype(f32) + swap(send, axis, bit).astype(f32)).astype(bf)]
    reduce_sum x7 -> x4, other arithmetic: 46.2 us -> 5.39 us  [the longest x1 2.5 us: on_device(): gsum = jnp.sum(cotangent.astype(f32), axis=(0, 1))]
  transfers between devices with their start and end apart: 5 -> 36, of which waited for: 4 -> 22; matrix products, arithmetic and copies ran while one was open for 24% -> 20% of each run, Pallas kernels for 0% -> 17%
where the time goes in v1:
time: 478 us; the launch traced here: 469 us
  waiting for transfers between devices  165 us (35%)
  Pallas kernels  132 us (28%)
  other arithmetic  66.2 us (14%)
  starting transfers between devices  53.7 us (11%)
  local copies, waits for them, and re-layouts  44.8 us (9%)
  matrix products  5.78 us (1%)
    ppermute x36, waiting for transfers between devices, swap(): return lax.ppermute(x, axis, [(i, i ^ bit) for i in range(n)])  165 us
    pallas_call x1, Pallas kernels, attention(): pl.pallas_call(attn_body, grid=(rows,), out_shape=(jax.ShapeDtypeStruct((...  68.5 us
    ppermute x36, starting transfers between devices, swap(): return lax.ppermute(x, axis, [(i, i ^ bit) for i in range(n)])  53.7 us
    pallas_call x1, Pallas kernels, mlp(): pl.pallas_call(mlp_body, out_shape=(jax.ShapeDtypeStruct((toks, d), bf),...  41.6 us
    another operation x5, other arithmetic, ag_step(): return jnp.stack([x, swap(x, axis, bit)])  15.6 us
    pallas_call x1, Pallas kernels, fill_mlp(): pl.pallas_call(fill_body, out_shape=(jax.ShapeDtypeStruct((d, nc * nx * d...  11.9 us
    pallas_call x1, Pallas kernels, fill_attn(): pl.pallas_call(fill_attn_body, out_shape=(jax.ShapeDtypeStruct((d, nc * n...  9.84 us
    select_n x6, other arithmetic, pair(): first = jnp.where(bit == 0, mine, other)  9.65 us
  transfers between devices with their start and end apart: 36, of which 22 were waited for; matrix products, arithmetic and copies ran while one was open for 20% of the time, Pallas kernels for 17%

profile of v1, /device:TPU:0, one launch (start us, length us, event | category | flops | bytes accessed | tf_op | source)
XLA Modules:
  0.0 469.4 jit_solution(9583149696734171233)
XLA Ops:
  1.2 2.6 collective-permute-start.1
  7.3 1.6 copy.83
  10.5 1.6 maximum_bitcast_fusion.1.cos_ref
  12.1 1.7 maximum_bitcast_fusion.2.sin_ref
  20.5 10.1 %collective-permute-done.1 = bf16[3,256,768]{2,1,0:T(8,128)(2,1)} collective-permute-done((bf16[3,256,768]{2,1,0:T(8,128)(2,1)}, bf16[3,256,768]{2,1,0:T(8,128)(2,1)}, u32[]{:S(2)}, u32[]{:S(2)}) %collective-permute-start.1) | collective-permute-done | bytes 1179680 | tf_op jit(solution)/shard_map/ppermute | solution.py:338
  30.6 4.4 constant_dynamic-slice_fusion.3
  35.0 4.7 copy.77
  39.7 1.8 collective-permute-start.4
  45.8 2.3 pad.15.w_ref
  48.7 2.8 broadcast_select_fusion.7
  51.6 4.2 collective-permute-done.4
  55.8 2.2 copy.79
  60.7 1.9 broadcast_select_fusion.5
  63.0 2.1 broadcast_select_fusion.1
  65.1 41.6 %mlp.1 = (bf16[1536,768]{1,0:T(8,128)(2,1)}, bf16[1536,768]{1,0:T(8,128)(2,1)}, bf16[2,768,768]{2,1,0:T(8,128)(2,1)}, bf16[1536,768]{1,0:T(8,128)(2,1)}, f32[1,1536]{1,0:T(1,128)}, /*index=5*/f32[8,768]{1,0:T(8,128)}) custom-call(s32[1]{0:T(128)} %bitcast.11.core_ref, bf16[1536,768]{1,0:T(8,128)(2,1)} %bitcast.172, bf16[1536,768]{1,0:T(8,128)(2,1)} %bitcast.169, ...), custom_call_target="tpu_custom_call" | custom-call | flops 21743271936 | bytes 31457280 | tf_op jit(solution)/shard_map/mlp/pallas_call | solution.py:110
  106.7 2.6 fusion.14
  109.3 1.6 copy.119
  110.9 1.8 collective-permute-start.25
  112.6 2.5 pad_maximum_fusion.x_ref
  115.1 68.5 %attention.1 = (bf16[3,1024,192]{2,1,0:T(8,128)(2,1)}, bf16[3,1024,768]{2,1,0:T(8,128)(2,1)}, bf16[576,768]{1,0:T(8,128)(2,1)}, f32[1,640]{1,0:T(1,128)}, f32[8,768]{1,0:T(8,128)}) custom-call(bf16[3,1024,768]{2,1,0:T(8,128)(2,1)} %pad_maximum_fusion.x_ref, bf16[3,1024,192]{2,1,0:T(8,128)(2,1)} %pad_maximum_fusion.8.do_ref, bf16[768,640]{1,0:T(8,128)(2,1)} %pad.15.w_ref, ...), custom_call_target="tpu_custom_call" | custom-call | flops 22649241600 | bytes 20971520 | tf_op jit(solution)/shard_map/attention/pallas_call | solution.py:295
  183.7 2.1 constant_dynamic-slice_fusion
  185.7 2.3 copy.85
  189.5 2.5 fusion.1
  194.7 1.6 collective-permute-start.26
  196.3 2.5 collective-permute-start.28
  198.9 4.5 fusion
  204.8 5.6 %collective-permute-done.26 = bf16[2,2,96,768]{3,2,0,1:T(8,128)(2,1)} collective-permute-done((bf16[2,2,96,768]{3,2,0,1:T(8,128)(2,1)}, bf16[2,2,96,768]{3,2,0,1:T(8,128)(2,1)}, u32[]{:S(2)}, u32[]{:S(2)}) %collective-permute-start.26) | collective-permute-done | bytes 589856 | tf_op jit(solution)/shard_map/ppermute | solution.py:338
  210.4 15.7 %collective-permute-done.28 = bf16[2,2,96,768]{3,2,0,1:T(8,128)(2,1)} collective-permute-done((bf16[2,2,96,768]{3,2,0,1:T(8,128)(2,1)}, bf16[2,2,96,768]{3,2,0,1:T(8,128)(2,1)}, u32[]{:S(2)}, u32[]{:S(2)}) %collective-permute-start.28) | collective-permute-done | bytes 589856 | tf_op jit(solution)/shard_map/ppermute | solution.py:338
  226.0 23.4 %collective-permute-done.27 = bf16[2,2,96,768]{3,2,0,1:T(8,128)(2,1)} collective-permute-done((bf16[2,2,96,768]{3,2,0,1:T(8,128)(2,1)}, bf16[2,2,96,768]{3,2,0,1:T(8,128)(2,1)}, u32[]{:S(2)}, u32[]{:S(2)}) %collective-permute-start.27) | collective-permute-done | bytes 589856 | tf_op jit(solution)/shard_map/ppermute | solution.py:338
  249.5 1.9 fusion.20
  252.6 6.0 %collective-permute-done.29 = bf16[2,96,768]{2,1,0:T(8,128)(2,1)S(1)} collective-permute-done((bf16[2,96,768]{2,1,0:T(8,128)(2,1)S(1)}, bf16[2,96,768]{2,1,0:T(8,128)(2,1)S(1)}, u32[]{:S(2)}, u32[]{:S(2)}) %collective-permute-start.29) | collective-permute-done | bytes 294944 | tf_op jit(solution)/shard_map/ppermute | solution.py:338
  262.0 1.6 dynamic-slice_bitcast_fusion
  263.6 4.5 collective-permute-done.30
  268.3 2.8 collective-permute-start.31
  273.5 24.1 %collective-permute-done.32 = bf16[2,2,96,768]{3,2,0,1:T(8,128)(2,1)S(1)} collective-permute-done((bf16[2,2,96,768]{3,2,0,1:T(8,128)(2,1)S(1)}, bf16[2,2,96,768]{3,2,0,1:T(8,128)(2,1)S(1)}, u32[]{:S(2)}, u32[]{:S(2)}) %collective-permute-start.32) | collective-permute-done | bytes 589856 | tf_op jit(solution)/shard_map/ppermute | solution.py:338
  297.6 8.2 %collective-permute-done.31 = bf16[2,2,96,768]{3,2,0,1:T(8,128)(2,1)S(1)} collective-permute-done((bf16[2,2,96,768]{3,2,0,1:T(8,128)(2,1)S(1)}, bf16[2,2,96,768]{3,2,0,1:T(8,128)(2,1)S(1)}, u32[]{:S(2)}, u32[]{:S(2)}) %collective-permute-start.31) | collective-permute-done | bytes 589856 | tf_op jit(solution)/shard_map/ppermute | solution.py:338
  305.8 1.6 fusion.36
  308.4 13.0 %collective-permute-start.11 = (bf16[96,768]{1,0:T(8,128)(2,1)S(1)}, bf16[96,768]{1,0:T(8,128)(2,1)S(1)}, u32[]{:S(2)}, u32[]{:S(2)}) collective-permute-start(bf16[96,768]{1,0:T(8,128)(2,1)S(1)} %get-tuple-element.86), channel_id=1, source_target_pairs={{0,8},{4,12},{8,0},{12,4},{16,24},{20,28},{24,16},{28,20},{1,9},{5... | collective-permute-start | bytes 442376 | tf_op jit(solution)/shard_map/ppermute | solution.py:338
  323.0 2.7 collective-permute-done.11
  325.7 4.6 collective-permute-done.13
  330.3 5.6 %collective-permute-done.12 = bf16[96,768]{1,0:T(8,128)(2,1)S(1)} collective-permute-done((bf16[96,768]{1,0:T(8,128)(2,1)S(1)}, bf16[96,768]{1,0:T(8,128)(2,1)S(1)}, u32[]{:S(2)}, u32[]{:S(2)}) %collective-permute-start.12) | collective-permute-done | bytes 147488 | tf_op jit(solution)/shard_map/ppermute | solution.py:338
  337.0 4.1 collective-permute-done.14
  342.0 1.9 collective-permute-start.15
  343.9 2.5 collective-permute-start.17
  347.1 11.0 %collective-permute-done.16 = bf16[2,96,768]{2,1,0:T(8,128)(2,1)} collective-permute-done((bf16[2,96,768]{2,1,0:T(8,128)(2,1)}, bf16[2,96,768]{2,1,0:T(8,128)(2,1)}, u32[]{:S(2)}, u32[]{:S(2)}) %collective-permute-start.16) | collective-permute-done | bytes 294944 | tf_op jit(solution)/shard_map/ppermute | solution.py:338
  358.1 4.2 collective-permute-done.15
  362.3 2.9 fusion.34
  366.7 2.9 fusion.2
  369.6 6.9 %fusion.35 = (bf16[1,2,4,2,2,96,768]{6,5,3,2,1,0,4:T(8,128)(2,1)}, bf16[2,4,2,2,96,768]{5,4,2,1,0,3:T(8,128)(2,1)}) fusion(bf16[1,4,2,2,96,768]{5,4,2,1,0,3:T(8,128)(2,1)} %bitcast.71, bf16[1,4,2,2,96,768]{5,4,2,1,0,3:T(8,128)(2,1)S(1)} %get-tuple-element.59), kind=kLoop, calls=%fused_computation.146 | loop fusion | flops 2359296 | bytes 14155776 | tf_op jit(solution)/shard_map/stack | solution.py:361
  379.2 3.2 add_convert_fusion
  384.5 6.5 %collective-permute-done.18 = bf16[4,2,96,768]{3,2,1,0:T(8,128)(2,1)} collective-permute-done((bf16[4,2,96,768]{3,2,1,0:T(8,128)(2,1)}, bf16[4,2,96,768]{3,2,1,0:T(8,128)(2,1)}, u32[]{:S(2)}, u32[]{:S(2)}) %collective-permute-start.18) | collective-permute-done | bytes 1179680 | tf_op jit(solution)/shard_map/ppermute | solution.py:338
  391.0 1.7 fusion.33
  392.8 13.5 %collective-permute-done.8 = bf16[3,256,768]{2,1,0:T(8,128)(2,1)} collective-permute-done((bf16[3,256,768]{2,1,0:T(8,128)(2,1)}, bf16[3,256,768]{2,1,0:T(8,128)(2,1)}, u32[]{:S(2)}, u32[]{:S(2)}) %collective-permute-start.8) | collective-permute-done | bytes 1179680 | tf_op jit(solution)/shard_map/ppermute | solution.py:338
  406.3 2.2 convert_reduce_fusion
  408.5 2.5 convert_reduce_fusion.2
  413.0 3.3 collective-permute-done.21
  416.9 3.4 collective-permute-done.22
  420.4 6.6 %collective-permute-start.23 = (f32[72,128]{1,0:T(8,128)S(1)}, f32[72,128]{1,0:T(8,128)S(1)}, u32[]{:S(2)}, u32[]{:S(2)}) collective-permute-start(f32[72,128]{1,0:T(8,128)S(1)} %add.217), channel_id=1, source_target_pairs={{0,8},{4,12},{8,0},{12,4},{16,24},{20,28},{24,16},{28,20},{1,9},{5... | collective-permute-start | bytes 110600 | tf_op jit(solution)/shard_map/ppermute | solution.py:338
  427.0 1.9 collective-permute-done.23
  428.9 3.0 collective-permute-start.24
  435.7 2.6 pad_maximum_fusion.1.pieces_ref
  438.3 9.8 %fill_attn.1 = (f32[768,2304]{1,0:T(8,128)}, f32[768,768]{1,0:T(8,128)}) custom-call(s32[4]{0:T(128)} %pad_add_fusion.own_ref, bf16[2,2,4,2,96,768]{5,4,3,2,1,0:T(8,128)(2,1)} %pad_maximum_fusion.1.pieces_ref), custom_call_target="tpu_custom_call" | custom-call | tf_op jit(solution)/shard_map/fill_attn/pallas_call | solution.py:431
  448.1 8.3 %maximum_bitcast_fusion.pieces_ref = bf16[2,2,2,4,2,96,768]{6,5,4,3,2,1,0:T(8,128)(2,1)} fusion(bf16[1,2,4,2,2,96,768]{6,5,3,2,1,0,4:T(8,128)(2,1)} %bitcast.74, bf16[1,2,4,2,2,96,768]{6,5,3,2,1,0,4:T(8,128)(2,1)} %get-tuple-element.53), kind=kLoop, calls=%fused_computation | loop fusion | flops 4718592 | bytes 18874368 | tf_op jit(solution)/shard_map/transpose | solution.py:486
  456.5 11.9 %fill_mlp.1 = (f32[768,3072]{1,0:T(8,128)}, f32[3072,768]{1,0:T(8,128)}) custom-call(s32[4]{0:T(128)} %pad_add_fusion.own_ref, bf16[2,2,2,4,2,96,768]{6,5,4,3,2,1,0:T(8,128)(2,1)} %maximum_bitcast_fusion.pieces_ref), custom_call_target="tpu_custom_call" | custom-call | tf_op jit(solution)/shard_map/fill_mlp/pallas_call | solution.py:401
  (190 shorter events, 51.4 us)
Async XLA Ops:
  0.6 4.3 copy-start
  0.7 48.1 %collective-permute-start = (bf16[3,256,768]{2,1,0:T(8,128)(2,1)}, bf16[3,256,768]{2,1,0:T(8,128)(2,1)}, u32[]{:S(2)}, u32[]{:S(2)}) collective-permute-start(bf16[3,256,768]{2,1,0:T(8,128)(2,1)} %param.15), channel_id=1, source_target_pairs={{0,1},{1,0},{2,3},{3,2},{4,5},{5,4},{6,7},{7,6},{8,9},{9,8},{10,11... | collective-permute-start | bytes 3538952 | tf_op jit(solution)/shard_map/ppermute | solution.py:338
  1.2 29.4 %collective-permute-start.1 = (bf16[3,256,768]{2,1,0:T(8,128)(2,1)}, bf16[3,256,768]{2,1,0:T(8,128)(2,1)}, u32[]{:S(2)}, u32[]{:S(2)}) collective-permute-start(bf16[3,256,768]{2,1,0:T(8,128)(2,1)} %param.15), channel_id=1, source_target_pairs={{0,2},{1,3},{2,0},{3,1},{4,6},{5,7},{6,4},{7,5},{8,10},{9,11},{10,... | collective-permute-start | bytes 3538952 | tf_op jit(solution)/shard_map/ppermute | solution.py:338
  3.7 10.1 %collective-permute-start.3 = (bf16[3,256,768]{2,1,0:T(8,128)(2,1)}, bf16[3,256,768]{2,1,0:T(8,128)(2,1)}, u32[]{:S(2)}, u32[]{:S(2)}) collective-permute-start(bf16[3,256,768]{2,1,0:T(8,128)(2,1)} %param.29), channel_id=1, source_target_pairs={{0,1},{1,0},{2,3},{3,2},{4,5},{5,4},{6,7},{7,6},{8,9},{9,8},{10,11... | collective-permute-start | bytes 3538952 | tf_op jit(solution)/shard_map/ppermute | solution.py:338
  15.3 2.8 copy-start.31
  20.4 22.4 %copy-start.26 = (bf16[768]{0:T(1024)(128)(2,1)S(1)}, bf16[768]{0:T(1024)(128)(2,1)}, u32[]{:S(2)}) copy-start(bf16[768]{0:T(1024)(128)(2,1)} %param.25) | copy-start | bytes 4612
  20.4 23.0 %copy-start.27 = (bf16[768]{0:T(1024)(128)(2,1)S(1)}, bf16[768]{0:T(1024)(128)(2,1)}, u32[]{:S(2)}) copy-start(bf16[768]{0:T(1024)(128)(2,1)} %param.26) | copy-start | bytes 4612
  20.5 23.5 %copy-start.28 = (bf16[768]{0:T(1024)(128)(2,1)S(1)}, bf16[768]{0:T(1024)(128)(2,1)}, u32[]{:S(2)}) copy-start(bf16[768]{0:T(1024)(128)(2,1)} %param.27) | copy-start | bytes 4612
  20.5 24.1 %copy-start.29 = (bf16[768]{0:T(1024)(128)(2,1)S(1)}, bf16[768]{0:T(1024)(128)(2,1)}, u32[]{:S(2)}) copy-start(bf16[768]{0:T(1024)(128)(2,1)} %param.28) | copy-start | bytes 4612
  20.5 24.7 %copy-start.23 = (bf16[3072]{0:T(1024)(128)(2,1)S(1)}, bf16[3072]{0:T(1024)(128)(2,1)}, u32[]{:S(2)}) copy-start(bf16[3072]{0:T(1024)(128)(2,1)} %param.22) | copy-start | bytes 18436
  30.6 30.1 %collective-permute-start.2 = (bf16[3,256,768]{2,1,0:T(8,128)(2,1)}, bf16[3,256,768]{2,1,0:T(8,128)(2,1)}, u32[]{:S(2)}, u32[]{:S(2)}) collective-permute-start(bf16[3,256,768]{2,1,0:T(8,128)(2,1)} %collective-permute-done.1), channel_id=1, source_target_pairs={{0,1},{1,0},{2,3},{3,2},{4,5},{5,4},{6,7},{7,6},{8,9},{9,8},{10,11... | collective-permute-start | bytes 3538952 | tf_op jit(solution)/shard_map/ppermute | solution.py:338
  35.0 13.7 %copy-start.2 = (bf16[3,256,768]{2,1,0:T(8,128)(2,1)S(1)}, bf16[3,256,768]{2,1,0:T(8,128)(2,1)}, u32[]{:S(2)}) copy-start(bf16[3,256,768]{2,1,0:T(8,128)(2,1)} %param.15) | copy-start | bytes 3538948
  39.7 16.1 %collective-permute-start.4 = (bf16[3,512,192]{1,2,0:T(8,128)(2,1)}, bf16[3,512,192]{1,2,0:T(8,128)(2,1)}, u32[]{:S(2)}, u32[]{:S(2)}) collective-permute-start(bf16[3,512,192]{1,2,0:T(8,128)(2,1)} %bitcast.183), channel_id=1, source_target_pairs={{0,2},{1,3},{2,0},{3,1},{4,6},{5,7},{6,4},{7,5},{8,10},{9,11},{10,... | collective-permute-start | bytes 1769480 | tf_op jit(solution)/shard_map/ppermute | solution.py:338
  60.7 2.3 copy-start.10
  110.9 78.7 %collective-permute-start.25 = (bf16[2,2,4,96,768]{4,3,0,1,2:T(8,128)(2,1)}, bf16[2,2,4,96,768]{4,3,0,1,2:T(8,128)(2,1)}, u32[]{:S(2)}, u32[]{:S(2)}) collective-permute-start(bf16[2,2,4,96,768]{4,3,0,1,2:T(8,128)(2,1)} %bitcast.156), channel_id=1, source_target_pairs={{0,4},{4,0},{8,12},{12,8},{16,20},{20,16},{24,28},{28,24},{1,5},{5... | collective-permute-start | bytes 7077896 | tf_op jit(solution)/shard_map/ppermute | solution.py:338
  188.0 15.3 %collective-permute-start.5 = (bf16[3,512,192]{1,2,0:T(8,128)(2,1)}, bf16[3,512,192]{1,2,0:T(8,128)(2,1)}, u32[]{:S(2)}, u32[]{:S(2)}) collective-permute-start(bf16[3,512,192]{1,2,0:T(8,128)(2,1)} %bitcast.184), channel_id=1, source_target_pairs={{0,2},{1,3},{2,0},{3,1},{4,6},{5,7},{6,4},{7,5},{8,10},{9,11},{10,... | collective-permute-start | bytes 1769480 | tf_op jit(solution)/shard_map/ppermute | solution.py:338
  189.5 9.4 %slice-start.2 = ((s8[4718592]{0:T(1024)(128)(4,1)}), s8[4194304]{0:T(1024)(128)(4,1)S(1)}, s32[]{:S(2)}) async-start(s8[4718592]{0:T(1024)(128)(4,1)} %bitcast.159), calls=%async_computation.2 | async-start | bytes 8388608
  189.5 9.4 %slice-start.3 = ((s8[4718592]{0:T(1024)(128)(4,1)}), s8[524288]{0:T(1024)(128)(4,1)S(1)}, s32[]{:S(2)}) async-start(s8[4718592]{0:T(1024)(128)(4,1)} %bitcast.159), calls=%async_computation.3 | async-start | bytes 1048576
  193.5 5.4 %copy-start.17 = (bf16[1536,768]{1,0:T(8,128)(2,1)S(1)}, bf16[1536,768]{1,0:T(8,128)(2,1)}, u32[]{:S(2)}) copy-start(bf16[1536,768]{1,0:T(8,128)(2,1)} %get-tuple-element.32) | copy-start | bytes 7077892
  194.7 15.7 %collective-permute-start.26 = (bf16[2,2,96,768]{3,2,0,1:T(8,128)(2,1)}, bf16[2,2,96,768]{3,2,0,1:T(8,128)(2,1)}, u32[]{:S(2)}, u32[]{:S(2)}) collective-permute-start(bf16[2,2,96,768]{3,2,0,1:T(8,128)(2,1)} %get-tuple-element.61), channel_id=1, source_target_pairs={{0,8},{4,12},{8,0},{12,4},{16,24},{20,28},{24,16},{28,20},{1,9},{5... | collective-permute-start | bytes 1769480 | tf_op jit(solution)/shard_map/ppermute | solution.py:338
  196.3 29.8 %collective-permute-start.28 = (bf16[2,2,96,768]{3,2,0,1:T(8,128)(2,1)}, bf16[2,2,96,768]{3,2,0,1:T(8,128)(2,1)}, u32[]{:S(2)}, u32[]{:S(2)}) collective-permute-start(bf16[2,2,96,768]{3,2,0,1:T(8,128)(2,1)} %get-tuple-element.62), channel_id=1, source_target_pairs={{0,24},{4,28},{8,16},{12,20},{16,8},{20,12},{24,0},{28,4},{1,25},{... | collective-permute-start | bytes 1769480 | tf_op jit(solution)/shard_map/ppermute | solution.py:338
  198.7 50.7 %collective-permute-start.27 = (bf16[2,2,96,768]{3,2,0,1:T(8,128)(2,1)}, bf16[2,2,96,768]{3,2,0,1:T(8,128)(2,1)}, u32[]{:S(2)}, u32[]{:S(2)}) collective-permute-start(bf16[2,2,96,768]{3,2,0,1:T(8,128)(2,1)} %get-tuple-element.63), channel_id=1, source_target_pairs={{0,16},{4,20},{8,24},{12,28},{16,0},{20,4},{24,8},{28,12},{1,17},{... | collective-permute-start | bytes 1769480 | tf_op jit(solution)/shard_map/ppermute | solution.py:338
  203.3 48.7 %copy-start.18 = (bf16[3,1024,192]{2,1,0:T(8,128)(2,1)S(1)}, bf16[3,1024,192]{2,1,0:T(8,128)(2,1)}, u32[]{:S(2)}) copy-start(bf16[3,1024,192]{2,1,0:T(8,128)(2,1)} %get-tuple-element.29) | copy-start | bytes 3538948
  251.4 7.2 %collective-permute-start.29 = (bf16[2,96,768]{2,1,0:T(8,128)(2,1)S(1)}, bf16[2,96,768]{2,1,0:T(8,128)(2,1)S(1)}, u32[]{:S(2)}, u32[]{:S(2)}) collective-permute-start(bf16[2,96,768]{2,1,0:T(8,128)(2,1)S(1)} %dynamic-slice_bitcast_fusion.7), channel_id=1, source_target_pairs={{0,2},{1,3},{2,0},{3,1},{4,6},{5,7},{6,4},{7,5},{8,10},{9,11},{10,... | collective-permute-start | bytes 884744 | tf_op jit(solution)/shard_map/ppermute | solution.py:338
  252.1 7.2 %copy-start.13 = (bf16[3,256,768]{2,1,0:T(8,128)(2,1)S(1)}, bf16[3,256,768]{2,1,0:T(8,128)(2,1)}, u32[]{:S(2)}) copy-start(bf16[3,256,768]{2,1,0:T(8,128)(2,1)} %copy-done.12) | copy-start | bytes 3538948
  252.1 7.2 %copy-start.15 = (bf16[3,256,768]{2,1,0:T(8,128)(2,1)S(1)}, bf16[3,256,768]{2,1,0:T(8,128)(2,1)}, u32[]{:S(2)}) copy-start(bf16[3,256,768]{2,1,0:T(8,128)(2,1)} %copy-done.14) | copy-start | bytes 3538948
  252.6 7.9 %copy-start.19 = (bf16[3,512,384]{2,1,0:T(8,128)(2,1)}, bf16[3,512,384]{2,1,0:T(8,128)(2,1)S(1)}, u32[]{:S(2)}) copy-start(bf16[3,512,384]{2,1,0:T(8,128)(2,1)S(1)} %pad_maximum_fusion.9) | copy-start | bytes 3538948
  258.6 3.4 slice-start
  258.7 3.4 slice-start.1
  258.7 9.4 %collective-permute-start.30 = (bf16[2,96,768]{2,1,0:T(8,128)(2,1)S(1)}, bf16[2,96,768]{2,1,0:T(8,128)(2,1)S(1)}, u32[]{:S(2)}, u32[]{:S(2)}) collective-permute-start(bf16[2,96,768]{2,1,0:T(8,128)(2,1)S(1)} %fusion.22), channel_id=1, source_target_pairs={{0,2},{1,3},{2,0},{3,1},{4,6},{5,7},{6,4},{7,5},{8,10},{9,11},{10,... | collective-permute-start | bytes 884744 | tf_op jit(solution)/shard_map/ppermute | solution.py:338
  260.5 12.2 %collective-permute-start.9 = (bf16[192,768]{1,0:T(8,128)(2,1)S(1)}, bf16[192,768]{1,0:T(8,128)(2,1)S(1)}, u32[]{:S(2)}, u32[]{:S(2)}) collective-permute-start(bf16[192,768]{1,0:T(8,128)(2,1)S(1)} %dynamic-slice_bitcast_fusion.8), channel_id=1, source_target_pairs={{0,2},{1,3},{2,0},{3,1},{4,6},{5,7},{6,4},{7,5},{8,10},{9,11},{10,... | collective-permute-start | bytes 884744 | tf_op jit(solution)/shard_map/ppermute | solution.py:338
  263.6 9.2 %copy-start.21 = (bf16[576,768]{1,0:T(8,128)(2,1)S(1)}, bf16[576,768]{1,0:T(8,128)(2,1)}, u32[]{:S(2)}) copy-start(bf16[576,768]{1,0:T(8,128)(2,1)} %get-tuple-element.33) | copy-start | bytes 2654212
  263.6 103.1 %collective-permute-start.7 = (bf16[3,2,256,768]{3,2,0,1:T(8,128)(2,1)}, bf16[3,2,256,768]{3,2,0,1:T(8,128)(2,1)}, u32[]{:S(2)}, u32[]{:S(2)}) collective-permute-start(bf16[3,2,256,768]{3,2,0,1:T(8,128)(2,1)} %dynamic-slice_bitcast_fusion), channel_id=1, source_target_pairs={{0,1},{1,0},{2,3},{3,2},{4,5},{5,4},{6,7},{7,6},{8,9},{9,8},{10,11... | collective-permute-start | bytes 7077896 | tf_op jit(solution)/shard_map/ppermute | solution.py:338
  268.2 29.4 %collective-permute-start.32 = (bf16[2,2,96,768]{3,2,0,1:T(8,128)(2,1)S(1)}, bf16[2,2,96,768]{3,2,0,1:T(8,128)(2,1)S(1)}, u32[]{:S(2)}, u32[]{:S(2)}) collective-permute-start(bf16[2,2,96,768]{3,2,0,1:T(8,128)(2,1)S(1)} %get-tuple-element.85), channel_id=1, source_target_pairs={{0,16},{4,20},{8,24},{12,28},{16,0},{20,4},{24,8},{28,12},{1,17},{... | collective-permute-start | bytes 1769480 | tf_op jit(solution)/shard_map/ppermute | solution.py:338
  268.3 37.5 %collective-permute-start.31 = (bf16[2,2,96,768]{3,2,0,1:T(8,128)(2,1)S(1)}, bf16[2,2,96,768]{3,2,0,1:T(8,128)(2,1)S(1)}, u32[]{:S(2)}, u32[]{:S(2)}) collective-permute-start(bf16[2,2,96,768]{3,2,0,1:T(8,128)(2,1)S(1)} %get-tuple-element.85), channel_id=1, source_target_pairs={{0,8},{4,12},{8,0},{12,4},{16,24},{20,28},{24,16},{28,20},{1,9},{5... | collective-permute-start | bytes 1769480 | tf_op jit(solution)/shard_map/ppermute | solution.py:338
  271.1 34.7 %collective-permute-start.33 = (bf16[2,2,96,768]{3,2,0,1:T(8,128)(2,1)S(1)}, bf16[2,2,96,768]{3,2,0,1:T(8,128)(2,1)S(1)}, u32[]{:S(2)}, u32[]{:S(2)}) collective-permute-start(bf16[2,2,96,768]{3,2,0,1:T(8,128)(2,1)S(1)} %get-tuple-element.85), channel_id=1, source_target_pairs={{0,24},{4,28},{8,16},{12,20},{16,8},{20,12},{24,0},{28,4},{1,25},{... | collective-permute-start | bytes 1769480 | tf_op jit(solution)/shard_map/ppermute | solution.py:338
  272.9 35.2 %collective-permute-start.10 = (bf16[4,96,768]{2,1,0:T(8,128)(2,1)S(1)}, bf16[4,96,768]{2,1,0:T(8,128)(2,1)S(1)}, u32[]{:S(2)}, u32[]{:S(2)}) collective-permute-start(bf16[4,96,768]{2,1,0:T(8,128)(2,1)S(1)} %dynamic-slice_bitcast_fusion.6), channel_id=1, source_target_pairs={{0,4},{4,0},{8,12},{12,8},{16,20},{20,16},{24,28},{28,24},{1,5},{5... | collective-permute-start | bytes 1769480 | tf_op jit(solution)/shard_map/ppermute | solution.py:338
  307.4 62.2 %collective-permute-start.34 = (bf16[4,2,2,96,768]{4,3,1,0,2:T(8,128)(2,1)}, bf16[4,2,2,96,768]{4,3,1,0,2:T(8,128)(2,1)}, u32[]{:S(2)}, u32[]{:S(2)}) collective-permute-start(bf16[4,2,2,96,768]{4,3,1,0,2:T(8,128)(2,1)} %get-tuple-element.60), channel_id=1, source_target_pairs={{0,4},{4,0},{8,12},{12,8},{16,20},{20,16},{24,28},{28,24},{1,5},{5... | collective-permute-start | bytes 7077896 | tf_op jit(solution)/shard_map/ppermute | solution.py:338
  308.1 38.3 %copy-start.30 = (bf16[768]{0:T(1024)(128)(2,1)S(1)}, bf16[768]{0:T(1024)(128)(2,1)}, u32[]{:S(2)}) copy-start(bf16[768]{0:T(1024)(128)(2,1)} %param.24) | copy-start | bytes 4612
  308.4 17.3 %collective-permute-start.11 = (bf16[96,768]{1,0:T(8,128)(2,1)S(1)}, bf16[96,768]{1,0:T(8,128)(2,1)S(1)}, u32[]{:S(2)}, u32[]{:S(2)}) collective-permute-start(bf16[96,768]{1,0:T(8,128)(2,1)S(1)} %get-tuple-element.86), channel_id=1, source_target_pairs={{0,8},{4,12},{8,0},{12,4},{16,24},{20,28},{24,16},{28,20},{1,9},{5... | collective-permute-start | bytes 442376 | tf_op jit(solution)/shard_map/ppermute | solution.py:338
  321.4 8.9 %collective-permute-start.13 = (bf16[96,768]{1,0:T(8,128)(2,1)S(1)}, bf16[96,768]{1,0:T(8,128)(2,1)S(1)}, u32[]{:S(2)}, u32[]{:S(2)}) collective-permute-start(bf16[96,768]{1,0:T(8,128)(2,1)S(1)} %get-tuple-element.87), channel_id=1, source_target_pairs={{0,24},{4,28},{8,16},{12,20},{16,8},{20,12},{24,0},{28,4},{1,25},{... | collective-permute-start | bytes 442376 | tf_op jit(solution)/shard_map/ppermute | solution.py:338
  322.7 13.1 %collective-permute-start.12 = (bf16[96,768]{1,0:T(8,128)(2,1)S(1)}, bf16[96,768]{1,0:T(8,128)(2,1)S(1)}, u32[]{:S(2)}, u32[]{:S(2)}) collective-permute-start(bf16[96,768]{1,0:T(8,128)(2,1)S(1)} %get-tuple-element.88), channel_id=1, source_target_pairs={{0,16},{4,20},{8,24},{12,28},{16,0},{20,4},{24,8},{28,12},{1,17},{... | collective-permute-start | bytes 442376 | tf_op jit(solution)/shard_map/ppermute | solution.py:338
  336.0 5.2 %collective-permute-start.14 = (bf16[96,768]{1,0:T(8,128)(2,1)S(1)}, bf16[96,768]{1,0:T(8,128)(2,1)S(1)}, u32[]{:S(2)}, u32[]{:S(2)}) collective-permute-start(bf16[96,768]{1,0:T(8,128)(2,1)S(1)} %fusion.28), channel_id=1, source_target_pairs={{0,2},{1,3},{2,0},{3,1},{4,6},{5,7},{6,4},{7,5},{8,10},{9,11},{10,... | collective-permute-start | bytes 442376 | tf_op jit(solution)/shard_map/ppermute | solution.py:338
  342.0 16.0 %collective-permute-start.16 = (bf16[2,96,768]{2,1,0:T(8,128)(2,1)}, bf16[2,96,768]{2,1,0:T(8,128)(2,1)}, u32[]{:S(2)}, u32[]{:S(2)}) collective-permute-start(bf16[2,96,768]{2,1,0:T(8,128)(2,1)} %get-tuple-element.90), channel_id=1, source_target_pairs={{0,16},{4,20},{8,24},{12,28},{16,0},{20,4},{24,8},{28,12},{1,17},{... | collective-permute-start | bytes 884744 | tf_op jit(solution)/shard_map/ppermute | solution.py:338
  342.0 20.3 %collective-permute-start.15 = (bf16[2,96,768]{2,1,0:T(8,128)(2,1)}, bf16[2,96,768]{2,1,0:T(8,128)(2,1)}, u32[]{:S(2)}, u32[]{:S(2)}) collective-permute-start(bf16[2,96,768]{2,1,0:T(8,128)(2,1)} %get-tuple-element.90), channel_id=1, source_target_pairs={{0,8},{4,12},{8,0},{12,4},{16,24},{20,28},{24,16},{28,20},{1,9},{5... | collective-permute-start | bytes 884744 | tf_op jit(solution)/shard_map/ppermute | solution.py:338
  343.9 18.4 %collective-permute-start.17 = (bf16[2,96,768]{2,1,0:T(8,128)(2,1)}, bf16[2,96,768]{2,1,0:T(8,128)(2,1)}, u32[]{:S(2)}, u32[]{:S(2)}) collective-permute-start(bf16[2,96,768]{2,1,0:T(8,128)(2,1)} %get-tuple-element.90), channel_id=1, source_target_pairs={{0,24},{4,28},{8,16},{12,20},{16,8},{20,12},{24,0},{28,4},{1,25},{... | collective-permute-start | bytes 884744 | tf_op jit(solution)/shard_map/ppermute | solution.py:338
  365.2 25.8 %collective-permute-start.18 = (bf16[4,2,96,768]{3,2,1,0:T(8,128)(2,1)}, bf16[4,2,96,768]{3,2,1,0:T(8,128)(2,1)}, u32[]{:S(2)}, u32[]{:S(2)}) collective-permute-start(bf16[4,2,96,768]{3,2,1,0:T(8,128)(2,1)} %get-tuple-element.83), channel_id=1, source_target_pairs={{0,4},{4,0},{8,12},{12,8},{16,20},{20,16},{24,28},{28,24},{1,5},{5... | collective-permute-start | bytes 3538952 | tf_op jit(solution)/shard_map/ppermute | solution.py:338
  369.6 6.9 %copy-start.3 = (bf16[3,2,256,768]{3,2,0,1:T(8,128)(2,1)}, bf16[3,2,256,768]{3,2,0,1:T(8,128)(2,1)S(1)}, u32[]{:S(2)}) copy-start(bf16[3,2,256,768]{3,2,0,1:T(8,128)(2,1)S(1)} %fusion.2) | copy-start | bytes 7077892
  376.5 2.1 copy-start.24
  376.5 2.7 copy-start.20
  376.5 71.7 %collective-permute-start.35 = (bf16[2,4,2,2,96,768]{5,4,2,1,0,3:T(8,128)(2,1)}, bf16[2,4,2,2,96,768]{5,4,2,1,0,3:T(8,128)(2,1)}, u32[]{:S(2)}, u32[]{:S(2)}) collective-permute-start(bf16[2,4,2,2,96,768]{5,4,2,1,0,3:T(8,128)(2,1)} %get-tuple-element.54), channel_id=1, source_target_pairs={{0,1},{1,0},{2,3},{3,2},{4,5},{5,4},{6,7},{7,6},{8,9},{9,8},{10,11... | collective-permute-start | bytes 14155784 | tf_op jit(solution)/shard_map/ppermute | solution.py:338
  377.6 28.7 %collective-permute-start.8 = (bf16[3,256,768]{2,1,0:T(8,128)(2,1)}, bf16[3,256,768]{2,1,0:T(8,128)(2,1)}, u32[]{:S(2)}, u32[]{:S(2)}) collective-permute-start(bf16[3,256,768]{2,1,0:T(8,128)(2,1)} %dynamic-slice_bitcast_fusion.1), channel_id=1, source_target_pairs={{0,2},{1,3},{2,0},{3,1},{4,6},{5,7},{6,4},{7,5},{8,10},{9,11},{10,... | collective-permute-start | bytes 3538952 | tf_op jit(solution)/shard_map/ppermute | solution.py:338
  382.4 8.5 %copy-start.11 = (bf16[1,4,2,96,768]{4,3,2,1,0:T(8,128)(2,1)S(1)}, bf16[1,4,2,96,768]{4,3,2,1,0:T(8,128)(2,1)}, u32[]{:S(2)}) copy-start(bf16[1,4,2,96,768]{4,3,2,1,0:T(8,128)(2,1)} %get-tuple-element.82) | copy-start | bytes 3538948
  382.5 26.0 %collective-permute-start.6 = (bf16[3,256,768]{2,1,0:T(8,128)(2,1)S(1)}, bf16[3,256,768]{2,1,0:T(8,128)(2,1)S(1)}, u32[]{:S(2)}, u32[]{:S(2)}) collective-permute-start(bf16[3,256,768]{2,1,0:T(8,128)(2,1)S(1)} %dynamic-slice_bitcast_fusion.2), channel_id=1, source_target_pairs={{0,1},{1,0},{2,3},{3,2},{4,5},{5,4},{6,7},{7,6},{8,9},{9,8},{10,11... | collective-permute-start | bytes 3538952 | tf_op jit(solution)/shard_map/ppermute | solution.py:338
  391.0 15.3 %copy-start.4 = (bf16[3,2,256,768]{3,2,0,1:T(8,128)(2,1)S(1)}, bf16[3,2,256,768]{3,2,0,1:T(8,128)(2,1)}, u32[]{:S(2)}) copy-start(bf16[3,2,256,768]{3,2,0,1:T(8,128)(2,1)} %copy-done.3) | copy-start | bytes 7077892
  392.7 15.8 %copy-start.8 = (bf16[3,256,768]{2,1,0:T(8,128)(2,1)S(1)}, bf16[3,256,768]{2,1,0:T(8,128)(2,1)}, u32[]{:S(2)}) copy-start(bf16[3,256,768]{2,1,0:T(8,128)(2,1)} %param.29) | copy-start | bytes 3538948
  392.7 43.0 %collective-permute-start.19 = (bf16[2,4,2,96,768]{4,3,2,1,0:T(8,128)(2,1)S(1)}, bf16[2,4,2,96,768]{4,3,2,1,0:T(8,128)(2,1)S(1)}, u32[]{:S(2)}, u32[]{:S(2)}) collective-permute-start(bf16[2,4,2,96,768]{4,3,2,1,0:T(8,128)(2,1)S(1)} %get-tuple-element.65), channel_id=1, source_target_pairs={{0,1},{1,0},{2,3},{3,2},{4,5},{5,4},{6,7},{7,6},{8,9},{9,8},{10,11... | collective-permute-start | bytes 7077896 | tf_op jit(solution)/shard_map/ppermute | solution.py:338
  411.1 1.3 collective-permute-start.20
  412.4 4.0 collective-permute-start.21
  416.3 4.0 collective-permute-start.22
  420.4 8.5 %collective-permute-start.23 = (f32[72,128]{1,0:T(8,128)S(1)}, f32[72,128]{1,0:T(8,128)S(1)}, u32[]{:S(2)}, u32[]{:S(2)}) collective-permute-start(f32[72,128]{1,0:T(8,128)S(1)} %add.217), channel_id=1, source_target_pairs={{0,8},{4,12},{8,0},{12,4},{16,24},{20,28},{24,16},{28,20},{1,9},{5... | collective-permute-start | bytes 110600 | tf_op jit(solution)/shard_map/ppermute | solution.py:338
  428.9 5.0 %collective-permute-start.24 = (f32[72,128]{1,0:T(8,128)S(1)}, f32[72,128]{1,0:T(8,128)S(1)}, u32[]{:S(2)}, u32[]{:S(2)}) collective-permute-start(f32[72,128]{1,0:T(8,128)S(1)} %add.218), channel_id=1, source_target_pairs={{0,16},{4,20},{8,24},{12,28},{16,0},{20,4},{24,8},{28,12},{1,17},{... | collective-permute-start | bytes 110600 | tf_op jit(solution)/shard_map/ppermute | solution.py:338
  434.5 33.9 %copy-start.22 = (f32[768]{0:T(1024)}, f32[768]{0:T(1024)S(1)}, u32[]{:S(2)}) copy-start(f32[768]{0:T(1024)S(1)} %get-tuple-element.123) | copy-start | bytes 9220
  456.4 12.5 %copy-start.1 = (bf16[768,2304]{1,0:T(8,128)(2,1)S(1)}, bf16[768,2304]{1,0:T(8,128)(2,1)}, u32[]{:S(2)}) copy-start(bf16[768,2304]{1,0:T(8,128)(2,1)} %param.17) | copy-start | bytes 10616836
  (8 other events, 12.1 us)
